TPU v7x, 128 devices: a whole 4x4x4 slice. The times are simulated.
128 devices in a mesh: ctx: 16 (over z, x), tp: 8 (over y, core).
Axes of the slice: x: 4, y: 4, z: 4, core: 2. Of those that a mesh axis runs over, the one named last changes fastest.
Arguments:
- projected: bfloat16 [3, 4096, 8192], P(None, 'ctx', 'tp'), may hold values from -6 to 6
- feat_weight: float32 [3, 3, 8192], P(None, None, 'tp'), may hold values from -3.5 to 3.5
- long_filter: float32 [128, 8192], P(None, 'tp'), may hold values from -0.5 to 0.5
- out_weight: bfloat16 [8192, 6144], P('tp', 'ctx'), may hold values from -0.0625 to 0.0625
- seg_lengths: int32 [32], replicated, may hold values from 1 to 512, 4096 in all
- cotangent: bfloat16 [4096, 6144], P(('ctx', 'tp')), may hold values from -6 to 6
Outputs:
- block_out: bfloat16 [4096, 6144], P(('ctx', 'tp'))
- grad_projected: bfloat16 [3, 4096, 8192], P(None, 'ctx', 'tp')
- grad_long_filter: float32 [128, 8192], P(None, 'tp')
- grad_short_filter: float32 [3, 3, 8192], P(None, None, 'tp')
Inputs may be any that keep to these rules, and one draw needn't show every extreme that they name: `seg_lengths`: lengths of the 32 packed segments; they sum to 4096, and the longest is exactly 512.
All inputs are finite; a program needn't handle non-finite values.
Results may differ from a plain program's by a relative error of at most 0.02.
Values may be sent and summed in bfloat16 or wider, within the bound.
A program may use at most 192 MiB of HBM per device.

v0:
```python
import jax
import jax.numpy as jnp
from jax import lax
from jax.sharding import PartitionSpec as P


def from_behind(x, axis, by):
    size = lax.axis_size(axis)
    pairs = [(i, i + by) for i in range(size) if 0 <= i + by < size]
    return lax.ppermute(x, axis, pairs)


def segment_ages(positions, seg_lengths):
    seg_starts = jnp.cumsum(seg_lengths) - seg_lengths
    earlier = jnp.where(seg_starts[None, :] <= positions[:, None], seg_starts[None, :], 0)
    return positions - jnp.max(earlier, axis=1)


def causal_mix(source, weights, seg_age, extent):
    count_out = seg_age.shape[0]
    running = jnp.zeros((count_out, source.shape[1]), jnp.float32)
    for offset in range(extent):
        window = source[extent - 1 - offset : extent - 1 - offset + count_out].astype(jnp.float32)
        running = running + jnp.where(
            (seg_age >= offset)[:, None], weights[offset][None, :] * window, 0.0
        )
    return running


def anticausal_mix(source, weights, later_age, extent, count_out):
    running = jnp.zeros((count_out, source.shape[1]), jnp.float32)
    for offset in range(extent):
        window = source[offset : offset + count_out].astype(jnp.float32)
        allowed = later_age[offset : offset + count_out] >= offset
        running = running + jnp.where(allowed[:, None], weights[offset][None, :] * window, 0.0)
    return running


def correlate(gradient, history, seg_age, extent):
    count_out = seg_age.shape[0]
    results = []
    for offset in range(extent):
        window = history[extent - 1 - offset : extent - 1 - offset + count_out].astype(jnp.float32)
        results.append(
            jnp.sum(
                jnp.where((seg_age >= offset)[:, None], gradient.astype(jnp.float32) * window, 0.0),
                axis=0,
            )
        )
    return jnp.stack(results)


def shards(projected, feat_weight, long_filter, out_weight, seg_lengths, cotangent):
    row_count = projected.shape[1]
    long_width = long_filter.shape[0]
    short_width = feat_weight.shape[1]
    reach_left = long_width + short_width - 2
    offset_start = lax.axis_index("ctx") * row_count
    left_age = segment_ages(
        offset_start - reach_left + jnp.arange(row_count + reach_left, dtype=jnp.int32), seg_lengths
    )
    seg_age = left_age[reach_left:]
    later_age = segment_ages(
        offset_start + jnp.arange(row_count + long_width - 1, dtype=jnp.int32), seg_lengths
    )
    prev_edge = from_behind(projected[:, row_count - reach_left :, :], "ctx", 1)
    extended = jnp.concatenate([prev_edge, projected], axis=1)
    wide_feats = jnp.stack(
        [
            causal_mix(
                extended[branch], feat_weight[branch], left_age[short_width - 1 :], short_width
            )
            for branch in range(3)
        ]
    )
    product_ext = (wide_feats[1] * wide_feats[2]).astype(jnp.bfloat16)
    feats = wide_feats[:, long_width - 1 :]
    history = extended[:, reach_left - (short_width - 1) :]
    filtered = causal_mix(product_ext, long_filter, seg_age, long_width)
    gated = (feats[0] * filtered).astype(jnp.bfloat16)
    cot_rows = lax.all_gather(cotangent, "tp", axis=0, tiled=True)
    terms = jnp.dot(
        gated,
        lax.all_gather(out_weight, "ctx", axis=1, tiled=True),
        preferred_element_type=jnp.float32,
    )
    summed = lax.psum_scatter(terms.astype(jnp.bfloat16), "tp", scatter_dimension=0, tiled=True)
    grad_gated = lax.dot_general(
        cot_rows,
        lax.all_gather(out_weight, "ctx", axis=1, tiled=True),
        (((1,), (1,)), ((), ())),
        preferred_element_type=jnp.float32,
    )
    grad_gated = grad_gated.astype(jnp.bfloat16)
    grad_long = (grad_gated * feats[0]).astype(jnp.bfloat16)
    grad_query = grad_gated.astype(jnp.float32) * filtered
    long_next = from_behind(grad_long[: long_width - 1], "ctx", -1)
    grad_product = anticausal_mix(
        jnp.concatenate([grad_long, long_next], axis=0),
        long_filter,
        later_age,
        long_width,
        row_count,
    )
    grad_taps = correlate(grad_long, product_ext, seg_age, long_width)
    grad_feats = jnp.stack([grad_query, grad_product * feats[2], grad_product * feats[1]])
    feat_next = from_behind(grad_feats[:, : short_width - 1], "ctx", -1)
    grad_ext = jnp.concatenate([grad_feats, feat_next], axis=1)
    grad_inputs = jnp.stack(
        [
            anticausal_mix(
                grad_ext[branch],
                feat_weight[branch],
                later_age[: row_count + short_width - 1],
                short_width,
                row_count,
            )
            for branch in range(3)
        ]
    ).astype(jnp.bfloat16)
    grad_short = jnp.stack(
        [
            correlate(grad_feats[branch], history[branch], seg_age, short_width)
            for branch in range(3)
        ]
    )
    taps_total, short_total = (
        lax.psum(grad_taps.astype(jnp.bfloat16), "ctx").astype(jnp.float32),
        lax.psum(grad_short.astype(jnp.bfloat16), "ctx").astype(jnp.float32),
    )
    norm_factor = (row_count * lax.axis_size("ctx")) ** (-0.5)
    return (summed, grad_inputs, taps_total * norm_factor, short_total * norm_factor)


def solution(mesh):
    return jax.shard_map(
        shards,
        mesh=mesh,
        in_specs=(
            P(None, "ctx", "tp"),
            P(None, None, "tp"),
            P(None, "tp"),
            P("tp", "ctx"),
            P(),
            P(("ctx", "tp"), None),
        ),
        out_specs=(
            P(("ctx", "tp"), None),
            P(None, "ctx", "tp"),
            P(None, "tp"),
            P(None, None, "tp"),
        ),
        check_vma=False,
    )
```

profile of v0, /device:TPU:0, one launch (start us, length us, event | category | flops | bytes accessed | tf_op | source)
XLA Modules:
  0.0 858.4 jit_solution(11542563090918964483)
XLA Ops:
  8.7 2.4 slice.2048
  11.1 3.5 collective-permute-start
  32.7 5.7 fusion.604
  38.4 6.4 fusion.3
  45.3 12.3 %fusion.85 = f32[256,1024]{1,0:T(8,128)} fusion(f32[1024]{0:T(1024)S(1)} %bitcast.465, f32[1024]{0:T(1024)} %bitcast.64, f32[1024]{0:T(1024)S(1)} %bitcast.491, f32[1024]{0:T(1024)S(1)} %bitcast.493, f32[1024]{0:T(1024)S(1)} %bitcast.495, f32[1024]{0:T(1024)} %bitcast.60, f32[1024]{0:T(1024)S(1)} %bitcast.467, f32[1024]{0:T(1024)S(1)} %bitcast.469, ...), kind=kLoop, calls=%fused_computation.634 | loop fusion | flops 51118080 | bytes 26951936 | tf_op jit(solution)/shard_map/add | solution.py:24
  57.5 84.4 %all-gather.3.cloned.1.call-done = bf16[1024,6144]{1,0:T(8,128)(2,1)} async-done(((bf16[1024,384]{1,0:T(8,128)(2,1)}), bf16[1024,6144]{1,0:T(8,128)(2,1)}) %all-gather.3.cloned.1.call-update) | async-done | bytes 12582928 | tf_op jit(solution)/shard_map/all_gather | solution.py:84
  141.9 12.5 %fusion.520 = (bf16[1024]{0:T(1024)(128)(2,1)S(1)}, bf16[1024]{0:T(1024)(128)(2,1)S(1)}, bf16[256,1024]{1,0:T(8,128)(2,1)S(1)}, f32[1,256,1024]{2,1,0:T(8,128)}, bf16[256,1024]{1,0:T(8,128)(2,1)}) fusion(pred[256]{0:T(512)(128)(4,1)} %get-tuple-element.496, bf16[383,1024]{1,0:T(8,128)(2,1)S(1)} %fusion.3, pred[256]{0:T(512)(128)(4,1)} %get-tuple-element.495, ...), kind=kOutput, calls=%fused_computation.1069 | convolution fusion | flops 3229874176 | bytes 22037760 | tf_op jit(solution)/shard_map/dot_general | solution.py:88
  155.7 3.2 fusion.546
  158.9 3.0 fusion.544
  161.9 3.0 fusion.542
  164.9 3.0 fusion.540
  167.9 3.0 fusion.538
  171.0 2.8 fusion.548
  174.0 2.9 fusion.536
  177.1 2.2 fusion.528
  181.8 2.4 fusion.524
  184.4 2.2 fusion.522
  189.2 2.2 fusion.530
  269.4 22.0 %stack.736 = bf16[128,1024]{1,0:T(8,128)(2,1)} concatenate(bf16[1,1024]{1,0:T(2,128)(2,1)} %stack.608, bf16[1,1024]{1,0:T(2,128)(2,1)} %stack.609, bf16[1,1024]{1,0:T(2,128)(2,1)} %stack.610, bf16[1,1024]{1,0:T(2,128)(2,1)} %stack.611, bf16[1,1024]{1,0:T(2,128)(2,1)} %stack.612, bf16[1,1024]{1,0:T(2,128)(2,1)} %stack.613, bf16[1,1024]{1,0:T(2,128)(2,1)} %stack.614, ...), dimensions={0} | concatenate | bytes 524288 | tf_op jit(solution)/shard_map/stack | solution.py:50
  291.5 2.5 fusion.664
  294.0 2.4 fusion.665
  296.4 2.5 fusion.666
  298.9 2.5 fusion.675
  301.3 2.4 fusion.684
  303.7 2.5 fusion.667
  306.2 2.4 fusion.668
  308.6 2.5 fusion.669
  311.0 2.4 fusion.670
  316.0 411.5 %fusion.587 = (bf16[1024]{0:T(1024)(128)(2,1)}, bf16[1024]{0:T(1024)(128)(2,1)}, bf16[1024]{0:T(1024)(128)(2,1)}, f32[256,1024]{1,0:T(8,128)}, f32[256,1024]{1,0:T(8,128)S(1)}) fusion(bf16[3,256,1024]{2,1,0:T(8,128)(2,1)S(1)} %copy-done, bf16[3,129,1024]{2,1,0:T(8,128)(2,1)S(1)} %copy-done.4, pred[256]{0:T(512)(128)(4,1)} %get-tuple-element.646, ...), kind=kLoop, calls=%fused_computation.1153 | loop fusion | flops 173798400 | bytes 54623488 | tf_op jit(solution)/shard_map/reduce_sum | solution.py:45
  727.5 25.4 %fusion.581 = (bf16[1024]{0:T(1024)(128)(2,1)}, bf16[1024]{0:T(1024)(128)(2,1)}, bf16[1024]{0:T(1024)(128)(2,1)}, bf16[1024]{0:T(1024)(128)(2,1)}, bf16[1024]{0:...) fusion(bf16[3,256,1024]{2,1,0:T(8,128)(2,1)S(1)} %copy-done, ...), kind=kLoop, calls=%fused_computation.1144 | loop fusion | flops 96200704 | bytes 53110016 | tf_op jit(solution)/shard_map/reduce_sum | solution.py:45
  753.9 9.4 %convolution_convert_fusion = bf16[256,6144]{1,0:T(8,128)(2,1)} fusion(bf16[1024,6144]{1,0:T(8,128)(2,1)} %all-gather.3.cloned.1.call-done, f32[256,1024]{1,0:T(8,128)S(1)} %get-tuple-element.146, f32[1,256,1024]{2,1,0:T(8,128)S(1)} %copy-done.174), kind=kOutput, calls=%fused_computation.269 | convolution fusion | flops 3223322624 | bytes 17825792 | tf_op jit(solution)/shard_map/dot_general | solution.py:82
  768.1 75.4 %psum.15 = bf16[3,3,1024]{2,1,0:T(4,128)(2,1)S(1)} all-reduce(bf16[3,3,1024]{2,1,0:T(4,128)(2,1)S(1)} %pad_maximum_fusion.6), channel_id=1, replica_groups=mesh['ctx'=16,'tp'=8] {'ctx'}, use_global_device_ids=true, to_apply=%region_142.143 | all-reduce | flops 9216 | bytes 36864 | tf_op jit(solution)/shard_map/psum | solution.py:129
  (557 shorter events, 119.0 us)
Async XLA Ops:
  7.2 18.2 %copy-start.82 = (f32[3,3,1024]{2,1,0:T(4,128)S(1)}, f32[3,3,1024]{2,1,0:T(4,128)}, u32[]{:S(2)}) copy-start(f32[3,3,1024]{2,1,0:T(4,128)} %param.7) | copy-start | bytes 110596
  7.2 18.8 %copy-start.17 = (f32[128,1024]{1,0:T(8,128)S(1)}, f32[128,1024]{1,0:T(8,128)}, u32[]{:S(2)}) copy-start(f32[128,1024]{1,0:T(8,128)} %param.8) | copy-start | bytes 1572868
  7.2 50.3 %all-gather.5.cloned.1.call-start = ((), (), s32[]{:S(2)}) async-start(), calls=%async_computation.3 | async-start | bytes 3538944 | tf_op jit(solution)/shard_map/all_gather | solution.py:81
  7.9 134.0 %all-gather.3.cloned.1.call-start = ((), (), s32[]{:S(2)}) async-start(), calls=%async_computation.1 | async-start | bytes 13369344 | tf_op jit(solution)/shard_map/all_gather | solution.py:84
  8.7 24.1 %copy-start = (bf16[3,256,1024]{2,1,0:T(8,128)(2,1)S(1)}, bf16[3,256,1024]{2,1,0:T(8,128)(2,1)}, u32[]{:S(2)}) copy-start(bf16[3,256,1024]{2,1,0:T(8,128)(2,1)} %param.6) | copy-start | bytes 4718596
  8.7 835.4 %all-reduce.2.cloned.1.call-start = ((), (), s32[]{:S(2)}) async-start(), calls=%async_computation.4 | async-start | bytes 524288 | tf_op jit(solution)/shard_map/psum | solution.py:128
  11.1 21.6 %collective-permute-start = (bf16[3,129,1024]{2,1,0:T(8,128)(2,1)}, bf16[3,129,1024]{2,1,0:T(8,128)(2,1)S(1)}, u32[]{:S(2)}, u32[]{:S(2)}) collective-permute-start(bf16[3,129,1024]{2,1,0:T(8,128)(2,1)} %slice.2048), channel_id=1, source_target_pairs={{0,8},{8,16},{16,24},{24,32},{32,40},{40,48},{48,56},{56,64},{64,7... | collective-permute-start | bytes 2377736 | tf_op jit(solution)/shard_map/ppermute | solution.py:10
  26.1 18.8 %copy-start.44 = (f32[1,1024]{1,0:T(1,128)}, f32[1,1024]{1,0:T(1,128)S(1)}, u32[]{:S(2)}) copy-start(f32[1,1024]{1,0:T(1,128)S(1)} %get-tuple-element.362) | copy-start | bytes 12292
  26.1 18.8 %copy-start.45 = (f32[1,1024]{1,0:T(1,128)}, f32[1,1024]{1,0:T(1,128)S(1)}, u32[]{:S(2)}) copy-start(f32[1,1024]{1,0:T(1,128)S(1)} %get-tuple-element.363) | copy-start | bytes 12292
  26.1 18.8 %copy-start.46 = (f32[1,1024]{1,0:T(1,128)}, f32[1,1024]{1,0:T(1,128)S(1)}, u32[]{:S(2)}) copy-start(f32[1,1024]{1,0:T(1,128)S(1)} %get-tuple-element.364) | copy-start | bytes 12292
  26.1 18.8 %copy-start.47 = (f32[1,1024]{1,0:T(1,128)}, f32[1,1024]{1,0:T(1,128)S(1)}, u32[]{:S(2)}) copy-start(f32[1,1024]{1,0:T(1,128)S(1)} %get-tuple-element.365) | copy-start | bytes 12292
  26.1 18.8 %copy-start.48 = (f32[1,1024]{1,0:T(1,128)}, f32[1,1024]{1,0:T(1,128)S(1)}, u32[]{:S(2)}) copy-start(f32[1,1024]{1,0:T(1,128)S(1)} %get-tuple-element.366) | copy-start | bytes 12292
  26.1 18.8 %copy-start.49 = (f32[1,1024]{1,0:T(1,128)}, f32[1,1024]{1,0:T(1,128)S(1)}, u32[]{:S(2)}) copy-start(f32[1,1024]{1,0:T(1,128)S(1)} %get-tuple-element.367) | copy-start | bytes 12292
  26.1 18.8 %copy-start.50 = (f32[1,1024]{1,0:T(1,128)}, f32[1,1024]{1,0:T(1,128)S(1)}, u32[]{:S(2)}) copy-start(f32[1,1024]{1,0:T(1,128)S(1)} %get-tuple-element.368) | copy-start | bytes 12292
  26.1 18.8 %copy-start.51 = (f32[1,1024]{1,0:T(1,128)}, f32[1,1024]{1,0:T(1,128)S(1)}, u32[]{:S(2)}) copy-start(f32[1,1024]{1,0:T(1,128)S(1)} %get-tuple-element.369) | copy-start | bytes 12292
  26.1 18.8 %copy-start.52 = (f32[1,1024]{1,0:T(1,128)}, f32[1,1024]{1,0:T(1,128)S(1)}, u32[]{:S(2)}) copy-start(f32[1,1024]{1,0:T(1,128)S(1)} %get-tuple-element.370) | copy-start | bytes 12292
  26.2 18.8 %copy-start.53 = (f32[1,1024]{1,0:T(1,128)}, f32[1,1024]{1,0:T(1,128)S(1)}, u32[]{:S(2)}) copy-start(f32[1,1024]{1,0:T(1,128)S(1)} %get-tuple-element.371) | copy-start | bytes 12292
  26.2 18.8 %copy-start.54 = (f32[1,1024]{1,0:T(1,128)}, f32[1,1024]{1,0:T(1,128)S(1)}, u32[]{:S(2)}) copy-start(f32[1,1024]{1,0:T(1,128)S(1)} %get-tuple-element.372) | copy-start | bytes 12292
  26.2 18.8 %copy-start.55 = (f32[1,1024]{1,0:T(1,128)}, f32[1,1024]{1,0:T(1,128)S(1)}, u32[]{:S(2)}) copy-start(f32[1,1024]{1,0:T(1,128)S(1)} %get-tuple-element.373) | copy-start | bytes 12292
  26.2 18.8 %copy-start.56 = (f32[1,1024]{1,0:T(1,128)}, f32[1,1024]{1,0:T(1,128)S(1)}, u32[]{:S(2)}) copy-start(f32[1,1024]{1,0:T(1,128)S(1)} %get-tuple-element.374) | copy-start | bytes 12292
  26.8 18.2 %copy-start.61 = (f32[1,1024]{1,0:T(1,128)}, f32[1,1024]{1,0:T(1,128)S(1)}, u32[]{:S(2)}) copy-start(f32[1,1024]{1,0:T(1,128)S(1)} %get-tuple-element.333) | copy-start | bytes 12292
  26.9 18.2 %copy-start.62 = (f32[1,1024]{1,0:T(1,128)}, f32[1,1024]{1,0:T(1,128)S(1)}, u32[]{:S(2)}) copy-start(f32[1,1024]{1,0:T(1,128)S(1)} %get-tuple-element.334) | copy-start | bytes 12292
  26.9 18.2 %copy-start.63 = (f32[1,1024]{1,0:T(1,128)}, f32[1,1024]{1,0:T(1,128)S(1)}, u32[]{:S(2)}) copy-start(f32[1,1024]{1,0:T(1,128)S(1)} %get-tuple-element.335) | copy-start | bytes 12292
  154.4 137.0 %collective-permute-start.1 = (bf16[127,1024]{1,0:T(8,128)(2,1)S(1)}, bf16[127,1024]{1,0:T(8,128)(2,1)S(1)}, u32[]{:S(2)}, u32[]{:S(2)}) collective-permute-start(bf16[127,1024]{1,0:T(8,128)(2,1)S(1)} %slice.2753), channel_id=1, source_target_pairs={{8,0},{16,8},{24,16},{32,24},{40,32},{48,40},{56,48},{64,56},{72,6... | collective-permute-start | bytes 780296 | tf_op jit(solution)/shard_map/ppermute | solution.py:10
  291.4 560.2 %reduce-scatter.2.cloned.1.call-start = ((), (), s32[]{:S(2)}) async-start(), calls=%async_computation.2 | async-start | bytes 3538944 | tf_op jit(solution)/shard_map/reduce_scatter | solution.py:87
  316.0 411.5 %copy-start.8 = (bf16[256,1024]{1,0:T(8,128)(2,1)S(1)}, bf16[256,1024]{1,0:T(8,128)(2,1)}, u32[]{:S(2)}) copy-start(bf16[256,1024]{1,0:T(8,128)(2,1)} %get-tuple-element.643) | copy-start | bytes 1572868
  316.0 411.5 %copy-start.10 = (f32[1,383,1024]{2,1,0:T(8,128)S(1)}, f32[1,383,1024]{2,1,0:T(8,128)}, u32[]{:S(2)}) copy-start(f32[1,383,1024]{2,1,0:T(8,128)} %get-tuple-element.154) | copy-start | bytes 4706308
  316.0 411.5 %copy-start.11 = (f32[1,383,1024]{2,1,0:T(8,128)S(1)}, f32[1,383,1024]{2,1,0:T(8,128)}, u32[]{:S(2)}) copy-start(f32[1,383,1024]{2,1,0:T(8,128)} %get-tuple-element.155) | copy-start | bytes 4706308
  316.0 411.5 %copy-start.12 = (f32[1,383,1024]{2,1,0:T(8,128)S(1)}, f32[1,383,1024]{2,1,0:T(8,128)}, u32[]{:S(2)}) copy-start(f32[1,383,1024]{2,1,0:T(8,128)} %get-tuple-element.156) | copy-start | bytes 4706308
  316.0 411.5 %copy-start.16 = (f32[256,1024]{1,0:T(8,128)S(1)}, f32[256,1024]{1,0:T(8,128)}, u32[]{:S(2)}) copy-start(f32[256,1024]{1,0:T(8,128)} %fusion.85) | copy-start | bytes 3145732
  727.5 26.4 %copy-start.174 = (f32[1,256,1024]{2,1,0:T(8,128)S(1)}, f32[1,256,1024]{2,1,0:T(8,128)}, u32[]{:S(2)}) copy-start(f32[1,256,1024]{2,1,0:T(8,128)} %get-tuple-element.148) | copy-start | bytes 3145732
  766.7 79.2 %collective-permute-start.2 = (f32[3,2,1024]{2,1,0:T(2,128)S(1)}, f32[3,2,1024]{2,1,0:T(2,128)S(1)}, u32[]{:S(2)}, u32[]{:S(2)}) collective-permute-start(f32[3,2,1024]{2,1,0:T(2,128)S(1)} %pad_maximum_fusion.4), channel_id=1, source_target_pairs={{8,0},{16,8},{24,16},{32,24},{40,32},{48,40},{56,48},{64,56},{72,6... | collective-permute-start | bytes 73736 | tf_op jit(solution)/shard_map/ppermute | solution.py:10
  (150 other events, 656.3 us)
Sparse Core Ops, SparseCore 0:
  9.7 30.2 all-gather.4
  42.1 99.7 all-gather.2
  291.5 85.3 all-reduce.1
  763.5 36.5 reduce-scatter.1
where the time goes:
time: 862 us; the launch traced here: 858 us
  other arithmetic  540 us (63%)
  local copies, waits for them, and re-layouts  111 us (13%)
  waiting for transfers between devices  86.8 us (10%)
  blocking collectives  75.4 us (9%)
  matrix products  21.8 us (3%)
  between operations  16.9 us (2%)
    reduce_sum x16, other arithmetic, correlate(): jnp.sum(jnp.where((seg_age >= offset)[:, None], gradient.astype(jnp.float...  473 us
    another operation x138, local copies, waits for them, and re-layouts, correlate(): return jnp.stack(results)  97.9 us
    all_gather x1, waiting for transfers between devices, shards(): lax.all_gather(out_weight, 'ctx', axis=1, tiled=True)  84.4 us
    psum x1, blocking collectives, shards(): lax.psum(grad_short.astype(jnp.bfloat16), 'ctx').astype(jnp.float32)  75.4 us
    concatenate x10, other arithmetic, shards(): jnp.concatenate([grad_long, long_next], axis=0)  22.4 us
  transfers between devices with their start and end apart: 7, of which 2 were waited for; matrix products, arithmetic and copies ran while one was open for 76% of the time, Pallas kernels for 0%

commit v1 on v0

v1 whole, which is shorter than its diff:
```python
import functools
import math

import jax
import jax.numpy as jnp
import numpy as np
from jax import lax
from jax.experimental import pallas as pl
from jax.experimental.pallas import tpu as pltpu
from jax.sharding import PartitionSpec as P

F32 = jnp.float32
BF16 = jnp.bfloat16
ROWS = 256
CH = 1024
LB = CH // 128
BLK = 16
FAR = 8
TOKENS = 4096
NSEG = 32
PAD = 16


def tables():
    turn = np.pi * (2 * np.arange(BLK) + 1) / (2 * BLK)

    def wave(at):
        return np.concatenate([np.cos(np.outer(turn, at)), -np.sin(np.outer(turn, at))])

    into = wave(np.arange(BLK))
    back = wave(np.arange(BLK) + BLK) / BLK
    back[BLK:] = -back[BLK:]
    taps = np.zeros((FAR * 2 * BLK, FAR * BLK))
    window = wave(np.arange(2 * BLK))
    for k in range(FAR):
        for d in range(1, 2 * BLK):
            if k * BLK + d < FAR * BLK:
                taps[k * 2 * BLK : (k + 1) * 2 * BLK, k * BLK + d] = window[:, d]
    each = np.eye(FAR)
    stack = np.stack([np.kron(each, into), np.kron(each, back), taps])
    return stack.astype(jnp.bfloat16), np.swapaxes(stack, 1, 2).astype(jnp.bfloat16)


def lanes(l):
    return pl.ds(pl.multiple_of(l * 128, 128), 128)


def rows_at(start, count):
    return pl.ds(pl.multiple_of(start, 8), count)


def find_ages(seg_ref, base, age_ref, room_ref):
    def chunk(i, carry):
        at = rows_at(i * 64, 64)
        pos = lax.broadcasted_iota(jnp.int32, (64, 128), 0) + (base - 128 + i * 64)

        def one(k, state):
            start, latest, after = state
            end = start + seg_ref[k]
            inside = pos >= start
            return end, jnp.where(inside, start, latest), jnp.where(inside, end, after)

        zero = jnp.zeros((64, 128), jnp.int32)
        _, latest, after = lax.fori_loop(0, NSEG, one, (jnp.int32(0), zero, zero))
        age_ref[at, :] = jnp.where(pos < TOKENS, pos - latest, -1)
        room_ref[at, :] = after - pos
        return carry

    lax.fori_loop(0, 8, chunk, 0)


def in_block(count):
    return lax.rem(lax.broadcasted_iota(jnp.int32, (count, 128), 0), BLK)


def load_inputs(proj_ref, jhalo_ref, pj):
    def lane(l, carry):
        for b in range(3):
            pj[b, l, 0:PAD, :] = jhalo_ref[b, :, lanes(l)].astype(F32)
            pj[b, l, PAD : PAD + ROWS, :] = proj_ref[b, :, lanes(l)].astype(F32)
        return carry

    lax.fori_loop(0, LB, lane, 0)


def features(pj, fw_ref, age_ref, room_ref, feats, xs, xv, prod, first, count):
    def step(at, carry):
        l, r0 = at // count, (first + at % count) * 64
        age = age_ref[rows_at(128 + r0, 64), :]
        inside = in_block(64)
        got = []
        for b in range(3):
            total = pj[b, l, rows_at(PAD + r0, 64), :] * fw_ref[b, 0:1, lanes(l)]
            for i in range(1, 3):
                window = pj[b, l, pl.ds(PAD + r0 - i, 64), :]
                total = total + jnp.where(age >= i, window, 0.0) * fw_ref[b, i : i + 1, lanes(l)]
            feats[b, l, rows_at(r0, 64), :] = total
            got.append(total)
        product = (got[1] * got[2]).astype(BF16)
        wide = product.astype(F32)
        xs[l, rows_at(PAD + r0, 64), :] = wide
        live = room_ref[rows_at(128 + r0, 64), :] >= BLK - inside
        xv[pl.ds(pl.multiple_of(128 + r0, 16), 64), lanes(l)] = jnp.where(live, wide, 0.0).astype(BF16)
        if prod is not None:
            prod[pl.ds(pl.multiple_of(r0, 16), 64), lanes(l)] = product
        return carry

    lax.fori_loop(0, LB * count, step, 0)


def mask_halo(phalo_ref, room_ref, xv):
    def step(at, carry):
        l, r0 = at // 2, (at % 2) * 64
        live = room_ref[rows_at(r0, 64), :] >= BLK - in_block(64)
        rows = pl.ds(pl.multiple_of(r0, 16), 64)
        xv[rows, lanes(l)] = jnp.where(live, phalo_ref[rows, lanes(l)].astype(F32), 0.0).astype(BF16)
        return carry

    lax.fori_loop(0, LB * 2, step, 0)


def transform(table, source, target, group):
    def step(c, carry):
        cols = pl.ds(pl.multiple_of(c * 256, 256), 256)
        target[group * 256 : (group + 1) * 256, cols] = jnp.dot(
            table, source[group * 128 : (group + 1) * 128, cols], preferred_element_type=F32
        )
        return carry

    lax.fori_loop(0, CH // 256, step, 0)


def far_forward(spec_x, spec_g, age_ref, spec_y):
    def outer(at, carry):
        l, ft = at // 2, at % 2
        g = [
            (spec_g[rows_at(k * 32 + ft * 8, 8), lanes(l)], spec_g[rows_at(k * 32 + 16 + ft * 8, 8), lanes(l)])
            for k in range(FAR)
        ]

        def inner(m, carry):
            reach = age_ref[pl.ds(128 + m * BLK - 1, 1), :]
            reach = jnp.broadcast_to(reach, (8, 128))
            re = jnp.zeros((8, 128), F32)
            im = jnp.zeros((8, 128), F32)
            for k in range(1, FAR + 1):
                live = reach >= BLK * (k - 1)
                base = (FAR + m - k) * 32 + ft * 8
                xr = jnp.where(live, spec_x[rows_at(base, 8), lanes(l)], 0.0)
                xi = jnp.where(live, spec_x[rows_at(base + 16, 8), lanes(l)], 0.0)
                gr, gi = g[k - 1]
                re = re + (gr * xr - gi * xi)
                im = im + (gr * xi + gi * xr)
            spec_y[rows_at(m * 32 + ft * 8, 8), lanes(l)] = re
            spec_y[rows_at(m * 32 + 16 + ft * 8, 8), lanes(l)] = -im
            return carry

        lax.fori_loop(0, ROWS // BLK, inner, 0)
        return carry

    lax.fori_loop(0, LB * 2, outer, 0)


def far_back(spec_z, spec_g, age_ref, spec_p):
    def outer(at, carry):
        l, ft = at // 2, at % 2
        g = [
            (spec_g[rows_at(k * 32 + ft * 8, 8), lanes(l)], spec_g[rows_at(k * 32 + 16 + ft * 8, 8), lanes(l)])
            for k in range(FAR)
        ]

        def inner(n, carry):
            re = jnp.zeros((8, 128), F32)
            im = jnp.zeros((8, 128), F32)
            for k in range(1, FAR + 1):
                reach = age_ref[pl.ds(128 + (n + k) * BLK - 1, 1), :]
                live = jnp.broadcast_to(reach, (8, 128)) >= BLK * (k - 1)
                base = (n + k) * 32 + ft * 8
                zr = jnp.where(live, spec_z[rows_at(base, 8), lanes(l)], 0.0)
                zi = jnp.where(live, spec_z[rows_at(base + 16, 8), lanes(l)], 0.0)
                gr, gi = g[k - 1]
                re = re + (gr * zr - gi * zi)
                im = im + (gr * zi + gi * zr)
            spec_p[rows_at(n * 32 + ft * 8, 8), lanes(l)] = re
            spec_p[rows_at(n * 32 + 16 + ft * 8, 8), lanes(l)] = -im
            return carry

        lax.fori_loop(0, ROWS // BLK, inner, 0)
        return carry

    lax.fori_loop(0, LB * 2, outer, 0)


def far_taps(spec_x, spec_z, age_ref, spec_q):
    def outer(at, carry):
        l, ft = at // 2, at % 2

        def inner(m, state):
            reach = jnp.broadcast_to(age_ref[pl.ds(128 + m * BLK - 1, 1), :], (8, 128))
            zr = spec_z[rows_at(m * 32 + ft * 8, 8), lanes(l)]
            zi = spec_z[rows_at(m * 32 + 16 + ft * 8, 8), lanes(l)]
            out = []
            for k in range(1, FAR + 1):
                live = reach >= BLK * (k - 1)
                base = (FAR + m - k) * 32 + ft * 8
                xr = jnp.where(live, spec_x[rows_at(base, 8), lanes(l)], 0.0)
                xi = jnp.where(live, spec_x[rows_at(base + 16, 8), lanes(l)], 0.0)
                re, im = state[2 * k - 2], state[2 * k - 1]
                out.append(re + (xr * zr - xi * zi))
                out.append(im + (xr * zi + xi * zr))
            return tuple(out)

        zero = jnp.zeros((8, 128), F32)
        state = lax.fori_loop(0, ROWS // BLK, inner, (zero,) * (2 * FAR))
        for k in range(FAR):
            spec_q[rows_at(k * 32 + ft * 8, 8), lanes(l)] = state[2 * k]
            spec_q[rows_at(k * 32 + 16 + ft * 8, 8), lanes(l)] = -state[2 * k + 1]
        return carry

    lax.fori_loop(0, LB * 2, outer, 0)


def inverse(table, source, target, groups):
    def step(c, carry):
        cols = pl.ds(pl.multiple_of(c * 256, 256), 256)
        for group in range(groups):
            target[group * 128 : (group + 1) * 128, cols] = jnp.dot(
                table, source[group * 256 : (group + 1) * 256, cols].astype(BF16), preferred_element_type=F32
            )
        return carry

    lax.fori_loop(0, CH // 256, step, 0)


def near_forward(xs, lf_ref, age_ref, wide, feats, filt, gated):
    def step(at, carry):
        l, r0 = at // 4, (at % 4) * 64
        age = age_ref[rows_at(128 + r0, 64), :]
        inside = in_block(64)
        near = jnp.minimum(age, inside)
        total = jnp.where(age > inside, wide[rows_at(r0, 64), lanes(l)], 0.0)
        for j in range(BLK):
            window = xs[l, pl.ds(PAD + r0 - j, 64), :]
            total = total + jnp.where(near >= j, window, 0.0) * lf_ref[j : j + 1, lanes(l)]
        filt[l, rows_at(r0, 64), :] = total
        gate = feats[0, l, rows_at(r0, 64), :] * total
        gated[pl.ds(pl.multiple_of(r0, 16), 64), lanes(l)] = gate.astype(BF16)
        return carry

    lax.fori_loop(0, LB * 4, step, 0)


def make_long(gg_ref, feats, age_ref, gs_, gv, first, count):
    def step(at, carry):
        l, r0 = at // count, (first + at % count) * 64
        rows = pl.ds(pl.multiple_of(r0, 16), 64)
        long = (gg_ref[rows, lanes(l)].astype(F32) * feats[0, l, rows_at(r0, 64), :]).astype(BF16).astype(F32)
        gs_[l, rows_at(r0, 64), :] = long
        live = age_ref[rows_at(128 + r0, 64), :] > in_block(64)
        gv[rows, lanes(l)] = jnp.where(live, long, 0.0).astype(BF16)
        return carry

    lax.fori_loop(0, LB * count, step, 0)


def mask_next(glhalo_ref, age_ref, gv):
    def step(at, carry):
        l, r0 = at // 2, (at % 2) * 64
        live = age_ref[rows_at(128 + ROWS + r0, 64), :] > in_block(64)
        long = glhalo_ref[pl.ds(pl.multiple_of(r0, 16), 64), lanes(l)].astype(F32)
        gv[pl.ds(pl.multiple_of(ROWS + r0, 16), 64), lanes(l)] = jnp.where(live, long, 0.0).astype(BF16)
        return carry

    lax.fori_loop(0, LB * 2, step, 0)


def near_back(gs_, xs, lf_ref, age_ref, room_ref, wide, gg_ref, filt, feats, gf, near_taps):
    def lane(l, carry):
        def step(i, sums):
            r0 = i * 64
            age = age_ref[rows_at(128 + r0, 64), :]
            room = room_ref[rows_at(128 + r0, 64), :]
            inside = in_block(64)
            near = jnp.minimum(age, inside)
            ahead = jnp.minimum(room, BLK - inside)
            here = gs_[l, rows_at(r0, 64), :]
            total = jnp.where(room >= BLK - inside, wide[rows_at(r0, 64), lanes(l)], 0.0)
            out = []
            for j in range(BLK):
                later = gs_[l, pl.ds(r0 + j, 64), :]
                total = total + jnp.where(ahead > j, later, 0.0) * lf_ref[j : j + 1, lanes(l)]
                window = xs[l, pl.ds(PAD + r0 - j, 64), :]
                both = jnp.where(near >= j, window, 0.0) * here
                out.append(sums[j] + jnp.sum(both.reshape(8, 8, 128), axis=0))
            grad = gg_ref[pl.ds(pl.multiple_of(r0, 16), 64), lanes(l)].astype(F32)
            gf[0, l, rows_at(r0, 64), :] = grad * filt[l, rows_at(r0, 64), :]
            gf[1, l, rows_at(r0, 64), :] = total * feats[2, l, rows_at(r0, 64), :]
            gf[2, l, rows_at(r0, 64), :] = total * feats[1, l, rows_at(r0, 64), :]
            return tuple(out)

        sums = lax.fori_loop(0, 4, step, (jnp.zeros((8, 128), F32),) * BLK)
        for j in range(BLK):
            near_taps[j : j + 1, lanes(l)] = jnp.sum(sums[j], axis=0, keepdims=True)
        return carry

    lax.fori_loop(0, LB, lane, 0)


def last_step(gf, pj, fw_ref, age_ref, room_ref, gproj_ref, short_ref):
    def lane(l, carry):
        def step(i, sums):
            r0 = i * 64
            age = age_ref[rows_at(128 + r0, 64), :]
            room = room_ref[rows_at(128 + r0, 64), :]
            out = []
            for b in range(3):
                here = gf[b, l, rows_at(r0, 64), :]
                total = here * fw_ref[b, 0:1, lanes(l)]
                for i_tap in range(3):
                    window = pj[b, l, pl.ds(PAD + r0 - i_tap, 64), :]
                    if i_tap:
                        later = gf[b, l, pl.ds(r0 + i_tap, 64), :]
                        total = total + jnp.where(room > i_tap, later, 0.0) * fw_ref[b, i_tap : i_tap + 1, lanes(l)]
                        window = jnp.where(age >= i_tap, window, 0.0)
                    out.append(sums[b * 3 + i_tap] + jnp.sum((here * window).reshape(8, 8, 128), axis=0))
                gproj_ref[b, pl.ds(pl.multiple_of(r0, 16), 64), lanes(l)] = total.astype(BF16)
            return tuple(out)

        sums = lax.fori_loop(0, 4, step, (jnp.zeros((8, 128), F32),) * 9)
        for at in range(9):
            short_ref[at : at + 1, lanes(l)] = jnp.sum(sums[at], axis=0, keepdims=True)
        return carry

    lax.fori_loop(0, LB, lane, 0)


def kernel_forward(
    base_ref, seg_ref, proj_ref, jhalo_ref, phalo_ref, fw_ref, lf_ref, tab_ref, tabt_ref,
    gated, feats, filt, spec_x, spec_g, xs, pj, age_ref, room_ref, xv, spec_y, wide, lfb,
):
    find_ages(seg_ref, base_ref[0], age_ref, room_ref)
    load_inputs(proj_ref, jhalo_ref, pj)
    xs[:, 0:PAD, :] = jnp.zeros((LB, PAD, 128), F32)
    features(pj, fw_ref, age_ref, room_ref, feats, xs, xv, None, 0, 4)
    mask_halo(phalo_ref, room_ref, xv)
    lfb[...] = lf_ref[...].astype(BF16)
    transform(tab_ref[2], lfb, spec_g, 0)
    for group in range(3):
        transform(tab_ref[0], xv, spec_x, group)
    far_forward(spec_x, spec_g, age_ref, spec_y)
    inverse(tabt_ref[1], spec_y, wide, 2)
    near_forward(xs, lf_ref, age_ref, wide, feats, filt, gated)


def kernel_back(
    gg_ref, glhalo_ref, lf_ref, tab_ref, tabt_ref, feats, filt, spec_x, spec_g, xs, age_ref, room_ref,
    gf, taps_ref, gs_, gv, spec_z, spec_p, spec_q, wide, near_taps,
):
    make_long(gg_ref, feats, age_ref, gs_, gv, 0, 4)
    gs_[:, ROWS : ROWS + PAD, :] = jnp.zeros((LB, PAD, 128), F32)
    mask_next(glhalo_ref, age_ref, gv)
    for group in range(3):
        transform(tab_ref[1], gv, spec_z, group)
    far_back(spec_z, spec_g, age_ref, spec_p)
    inverse(tabt_ref[0], spec_p, wide, 2)
    far_taps(spec_x, spec_z, age_ref, spec_q)
    near_back(gs_, xs, lf_ref, age_ref, room_ref, wide, gg_ref, filt, feats, gf, near_taps)
    inverse(tabt_ref[2], spec_q, taps_ref, 1)
    taps_ref[0:BLK, :] = taps_ref[0:BLK, :] + near_taps[...]


def kernel_last(gf_ref, gfhalo_ref, pj, fw_ref, age_ref, room_ref, gproj_ref, short_ref, gf):
    gf[:, :, 0:ROWS, :] = gf_ref[...]
    gf[:, :, ROWS : ROWS + 8, :] = gfhalo_ref[...]
    last_step(gf, pj, fw_ref, age_ref, room_ref, gproj_ref, short_ref)


def call(kernel, outs, scratch, smem, args):
    vm = pl.BlockSpec(memory_space=pltpu.VMEM)
    sm = pl.BlockSpec(memory_space=pltpu.SMEM)
    return pl.pallas_call(
        kernel,
        out_shape=[jax.ShapeDtypeStruct(s, d) for s, d in outs],
        in_specs=[sm] * smem + [vm] * (len(args) - smem),
        out_specs=[vm] * len(outs),
        scratch_shapes=[pltpu.VMEM(s, d) for s, d in scratch],
        compiler_params=pltpu.CompilerParams(vmem_limit_bytes=56 * 2**20),
    )(*args)


SPEC = ((3 * 256, CH), F32)
AGE = ((512, 128), jnp.int32)
LANED = ((LB, ROWS, 128), F32)


def forward_call(base, seg, proj, jhalo, phalo, fw, lf, tab, tabt):
    return call(
        kernel_forward,
        [((ROWS, CH), BF16), ((3,) + LANED[0], F32), LANED, SPEC, ((256, CH), F32),
         ((LB, PAD + ROWS, 128), F32), ((3, LB, PAD + ROWS, 128), F32), AGE, AGE],
        [((128 + ROWS, CH), BF16), ((512, CH), F32), ((ROWS, CH), F32), ((128, CH), BF16)],
        2,
        (base, seg, proj, jhalo, phalo, fw, lf, tab, tabt),
    )


def back_call(*args):
    return call(
        kernel_back,
        [((3,) + LANED[0], F32), ((128, CH), F32)],
        [((LB, ROWS + PAD, 128), F32), ((ROWS + 128, CH), BF16), SPEC, ((512, CH), F32), ((256, CH), F32),
         ((ROWS, CH), F32), ((BLK, CH), F32)],
        0,
        args,
    )


def last_call(*args):
    return call(
        kernel_last,
        [((3, ROWS, CH), BF16), ((9, CH), F32)],
        [((3, LB, ROWS + PAD, 128), F32)],
        0,
        args,
    )


def from_behind(x, axis, by):
    size = lax.axis_size(axis)
    pairs = [(i, i + by) for i in range(size) if 0 <= i + by < size]
    return lax.ppermute(x, axis, pairs)


def segment_ages(positions, seg_lengths):
    seg_starts = jnp.cumsum(seg_lengths) - seg_lengths
    earlier = jnp.where(seg_starts[None, :] <= positions[:, None], seg_starts[None, :], 0)
    return positions - jnp.max(earlier, axis=1)


def shards(projected, feat_weight, long_filter, out_weight, seg_lengths, cotangent):
    tab, tabt = (jnp.asarray(t) for t in tables())
    base = lax.axis_index("ctx") * ROWS
    cot_rows = lax.all_gather(cotangent, "tp", axis=0, tiled=True)
    weight = lax.all_gather(out_weight, "ctx", axis=1, tiled=True)
    jhalo = from_behind(projected[:, ROWS - 16 :, :], "ctx", 1)
    tail_age = segment_ages(base + 128 + jnp.arange(128, dtype=jnp.int32), seg_lengths)
    tail = []
    for b in (1, 2):
        total = 0.0
        for i in range(3):
            window = projected[b, 128 - i : 256 - i].astype(F32)
            total = total + jnp.where((tail_age >= i)[:, None], window * feat_weight[b, i][None, :], 0.0)
        tail.append(total)
    phalo = from_behind((tail[0] * tail[1]).astype(BF16), "ctx", 1)
    gated, feats, filt, spec_x, spec_g, xs, pj, age, room = forward_call(
        base.reshape(1), seg_lengths, projected, jhalo, phalo, feat_weight, long_filter, tab, tabt
    )
    grad_gated = lax.dot_general(cot_rows, weight, (((1,), (1,)), ((), ())), preferred_element_type=F32)
    grad_gated = grad_gated.astype(BF16)
    front = jnp.swapaxes(feats[0, :, :128, :], 0, 1).reshape(128, CH)
    glhalo = from_behind((grad_gated[:128] * front).astype(BF16), "ctx", -1)
    terms = jnp.dot(gated, weight, preferred_element_type=F32)
    summed = lax.psum_scatter(terms.astype(BF16), "tp", scatter_dimension=0, tiled=True)
    gf, taps = back_call(
        grad_gated, glhalo, long_filter, tab, tabt, feats, filt, spec_x, spec_g, xs, age, room
    )
    gfhalo = from_behind(gf[:, :, :8, :], "ctx", -1)
    grad_inputs, short = last_call(gf, gfhalo, pj, feat_weight, age, room)
    norm = TOKENS**-0.5
    both = jnp.concatenate([taps, jnp.pad(short, ((0, 7), (0, 0)))], axis=0).astype(BF16)
    both = lax.psum(both, "ctx").astype(F32) * norm
    return (summed, grad_inputs, both[:128], both[128:137].reshape(3, 3, CH))


def solution(mesh):
    return jax.shard_map(
        shards,
        mesh=mesh,
        in_specs=(
            P(None, "ctx", "tp"),
            P(None, None, "tp"),
            P(None, "tp"),
            P("tp", "ctx"),
            P(),
            P(("ctx", "tp"), None),
        ),
        out_specs=(
            P(("ctx", "tp"), None),
            P(None, "ctx", "tp"),
            P(None, "tp"),
            P(None, None, "tp"),
        ),
        check_vma=False,
    )
```

time: 862 us -> 346 us (0.40)
  other arithmetic: 540 us -> 8.29 us
  waiting for transfers between devices: 86.8 us -> 219 us
  local copies, waits for them, and re-layouts: 111 us -> 6.99 us
  blocking collectives: 75.4 us -> 0 us
  Pallas kernels: 0 us -> 69.3 us
    reduce_sum x16 -> x0, other arithmetic: 473 us -> none  [correlate(): jnp.sum(jnp.where((seg_age >= offset)[:, None], gradient.astype(jnp.float...]
    another operation x139 -> x1, local copies, waits for them, and re-layouts: 98 us -> 0.74 us  [the longest x138 97.9 us: correlate(): return jnp.stack(results)]
    psum x1, waiting for transfers between devices: 0.01 us -> 77.6 us  [shards(): both = lax.psum(both, 'ctx').astype(F32) * norm]
    psum x1 -> x0, blocking collectives: 75.4 us -> none  [shards(): lax.psum(grad_short.astype(jnp.bfloat16), 'ctx').astype(jnp.float32)]
    pallas_call x0 -> x3, Pallas kernels: none -> 69.3 us  [call(): pl.pallas_call(kernel, out_shape=[jax.ShapeDtypeStruct(s, d) for s, d in...]
    reduce_scatter x1, waiting for transfers between devices: 0.01 us -> 34.7 us  [shards(): lax.psum_scatter(terms.astype(BF16), 'tp', scatter_dimension=0, tiled=True)]
    concatenate x11 -> x1, other arithmetic: 24 us -> 0.74 us  [shards(): jnp.concatenate([taps, jnp.pad(short, ((0, 7), (0, 0)))], axis=0)]
    ppermute x3 -> x4, waiting for transfers between devices: 1.01 us -> 15.3 us  [from_behind(): return lax.ppermute(x, axis, pairs)]
  transfers between devices with their start and end apart: 7 -> 8, of which waited for: 2 -> 6; matrix products, arithmetic and copies ran while one was open for 76% -> 5% of each run, Pallas kernels for 0% -> 8%
where the time goes in v1:
time: 346 us; the launch traced here: 345 us
  waiting for transfers between devices  219 us (63%)
  Pallas kernels  69.3 us (20%)
  matrix products  18.3 us (5%)
  between operations  13.9 us (4%)
  starting transfers between devices  9.6 us (3%)
  other arithmetic  8.29 us (2%)
  local copies, waits for them, and re-layouts  6.99 us (2%)
    all_gather x1, waiting for transfers between devices, shards(): weight = lax.all_gather(out_weight, 'ctx', axis=1, tiled=True)  89.7 us
    psum x1, waiting for transfers between devices, shards(): both = lax.psum(both, 'ctx').astype(F32) * norm  77.6 us
    pallas_call x3, Pallas kernels, call(): pl.pallas_call(kernel, out_shape=[jax.ShapeDtypeStruct(s, d) for s, d in...  69.3 us
    reduce_scatter x1, waiting for transfers between devices, shards(): lax.psum_scatter(terms.astype(BF16), 'tp', scatter_dimension=0, tiled=True)  34.7 us
    ppermute x4, waiting for transfers between devices, from_behind(): return lax.ppermute(x, axis, pairs)  15.3 us
    ppermute x4, starting transfers between devices, from_behind(): return lax.ppermute(x, axis, pairs)  9.44 us
    dot_general x1, matrix products, shards(): terms = jnp.dot(gated, weight, preferred_element_type=F32)  9.37 us
    dot_general x1, matrix products, shards(): lax.dot_general(cot_rows, weight, (((1,), (1,)), ((), ())), preferred_ele...  8.97 us
  transfers between devices with their start and end apart: 8, of which 6 were waited for; matrix products, arithmetic and copies ran while one was open for 5% of the time, Pallas kernels for 8%

profile of v1, /device:TPU:0, one launch (start us, length us, event | category | flops | bytes accessed | tf_op | source)
XLA Modules:
  0.0 345.0 jit_solution(6089114769803939012)
XLA Ops:
  7.2 0.7 all-gather.5.cloned.1.call-update
  7.9 0.7 all-gather.3.cloned.1.call-update
  8.7 0.7 copy.16
  9.6 0.7 sub.16
  10.4 0.9 fusion.16
  11.3 2.4 fusion.5
  13.7 3.5 %collective-permute-start.1 = (bf16[128,1024]{1,0:T(8,128)(2,1)S(1)}, bf16[128,1024]{1,0:T(8,128)(2,1)S(1)}, u32[]{:S(2)}, u32[]{:S(2)}) collective-permute-start(bf16[128,1024]{1,0:T(8,128)(2,1)S(1)} %fusion.5), channel_id=1, source_target_pairs={{0,8},{8,16},{16,24},{24,32},{32,40},{40,48},{48,56},{56,64},{64,7... | collective-permute-start | bytes 786440 | tf_op jit(solution)/shard_map/ppermute | solution.py:431
  17.2 0.9 slice.54
  18.1 3.4 collective-permute-start
  21.5 3.3 collective-permute-done.jhalo_ref
  25.6 26.7 %shard_map.111 = (bf16[256,1024]{1,0:T(8,128)(2,1)}, f32[3,8,256,128]{3,2,1,0:T(8,128)}, f32[8,256,128]{2,1,0:T(8,128)}, f32[768,1024]{1,0:T(8,128)}, f32[256,10...) custom-call(s32[1]{0:T(128)} %bitcast.base_ref, ...), custom_call_target="tpu_custom_call" | custom-call | tf_op jit(solution)/shard_map/pallas_call | solution.py:381
  52.3 89.7 %all-gather.3.cloned.1.call-done = bf16[1024,6144]{1,0:T(8,128)(2,1)} async-done(((bf16[1024,384]{1,0:T(8,128)(2,1)}), bf16[1024,6144]{1,0:T(8,128)(2,1)}) %all-gather.3.cloned.1.call-update) | async-done | bytes 12582928 | tf_op jit(solution)/shard_map/all_gather | solution.py:444
  142.0 9.0 %convolution_convert_fusion.1.gg_ref = bf16[256,1024]{1,0:T(8,128)(2,1)S(1)} fusion(bf16[256,6144]{1,0:T(8,128)(2,1)} %all-gather.5.cloned.1.call-done, bf16[1024,6144]{1,0:T(8,128)(2,1)} %all-gather.3.cloned.1.call-done), kind=kOutput, calls=%fused_computation.1 | convolution fusion | flops 3221487616 | bytes 16252928 | tf_op jit(solution)/shard_map/dot_general | solution.py:458
  151.0 1.3 fusion.1
  152.3 1.3 collective-permute-start.2
  153.6 7.8 %collective-permute-done.2.glhalo_ref = bf16[128,1024]{1,0:T(8,128)(2,1)S(1)} collective-permute-done((bf16[128,1024]{1,0:T(8,128)(2,1)S(1)}, bf16[128,1024]{1,0:T(8,128)(2,1)S(1)}, u32[]{:S(2)}, u32[]{:S(2)}) %collective-permute-start.2) | collective-permute-done | bytes 262176 | tf_op jit(solution)/shard_map/ppermute | solution.py:431
  161.4 0.7 copy-done.1
  162.1 35.9 %shard_map.112 = (f32[3,8,256,128]{3,2,1,0:T(8,128)}, f32[128,1024]{1,0:T(8,128)}) custom-call(bf16[256,1024]{1,0:T(8,128)(2,1)} %copy-done, bf16[128,1024]{1,0:T(8,128)(2,1)} %copy-done.1, f32[128,1024]{1,0:T(8,128)} %lf_ref.3, bf16[3,256,128]{2,1,0:T(8,128)(2,1)} %constant.33.clone.tab_ref, bf16[3,128,256]{2,1,0:T(8,128)(2,1)} %constant.34.clone.tabt_ref, ...), custom_call_target="tpu_custom_call" | custom-call | tf_op jit(solution)/shard_map/pallas_call | solution.py:381
  198.0 0.9 slice.69
  198.9 1.3 collective-permute-start.3
  200.2 1.1 convert.14
  201.2 4.1 %collective-permute-done.3.gfhalo_ref = f32[3,8,8,128]{3,2,1,0:T(8,128)S(1)} collective-permute-done((f32[3,8,8,128]{3,2,1,0:T(8,128)S(1)}, f32[3,8,8,128]{3,2,1,0:T(8,128)S(1)}, u32[]{:S(2)}, u32[]{:S(2)}) %collective-permute-start.3) | collective-permute-done | bytes 98336 | tf_op jit(solution)/shard_map/ppermute | solution.py:431
  205.4 0.6 copy-done.3
  206.0 6.7 %shard_map.113 = (bf16[3,256,1024]{2,1,0:T(8,128)(2,1)}, f32[9,1024]{1,0:T(8,128)}) custom-call(f32[3,8,256,128]{3,2,1,0:T(8,128)} %get-tuple-element.25.gf_ref, f32[3,8,8,128]{3,2,1,0:T(8,128)} %copy-done.3, f32[3,8,272,128]{3,2,1,0:T(8,128)} %get-tuple-element.26.pj, f32[3,3,1024]{2,1,0:T(4,128)} %fw_ref.3, s32[512,128]{1,0:T(8,128)} %get-tuple-element.23.age_ref, ...), custom_call_target="tpu_custom_call" | custom-call | tf_op jit(solution)/shard_map/pallas_call | solution.py:381
  212.7 0.8 convert.15
  213.5 0.7 fusion.14
  214.4 9.4 %convolution_convert_fusion = bf16[256,6144]{1,0:T(8,128)(2,1)} fusion(bf16[256,1024]{1,0:T(8,128)(2,1)S(1)} %copy-done.5, bf16[1024,6144]{1,0:T(8,128)(2,1)} %all-gather.3.cloned.1.call-done), kind=kOutput, calls=%fused_computation | convolution fusion | flops 3222798336 | bytes 16252928 | tf_op jit(solution)/shard_map/dot_general | solution.py:462
  223.8 77.6 %all-reduce.3.cloned.1.call-done = bf16[144,1024]{1,0:T(8,128)(2,1)} async-done(((bf16[144,1024]{1,0:T(8,128)(2,1)}), bf16[144,1024]{1,0:T(8,128)(2,1)}) %all-reduce.3.cloned.1.call-update) | async-done | bytes 294928 | tf_op jit(solution)/shard_map/psum | solution.py:471
  301.3 1.0 convert_multiply_fusion
  302.3 0.8 slice.73
  303.2 0.6 reshape.86
  303.8 34.7 %reduce-scatter.2.cloned.1.call-done = bf16[32,6144]{1,0:T(8,128)(2,1)} async-done(((bf16[256,6144]{1,0:T(8,128)(2,1)}), bf16[32,6144]{1,0:T(8,128)(2,1)}) %reduce-scatter.2.cloned.1.call-update) | async-done | bytes 393232 | tf_op jit(solution)/shard_map/reduce_scatter | solution.py:463
  (24 shorter events, 1.2 us)
Async XLA Ops:
  7.2 45.2 %all-gather.5.cloned.1.call-start = ((), (), s32[]{:S(2)}) async-start(), calls=%async_computation.3 | async-start | bytes 3538944 | tf_op jit(solution)/shard_map/all_gather | solution.py:443
  7.9 134.1 %all-gather.3.cloned.1.call-start = ((), (), s32[]{:S(2)}) async-start(), calls=%async_computation.1 | async-start | bytes 13369344 | tf_op jit(solution)/shard_map/all_gather | solution.py:444
  8.6 292.7 %all-reduce.3.cloned.1.call-start = ((), (), s32[]{:S(2)}) async-start(), calls=%async_computation.4 | async-start | bytes 589824 | tf_op jit(solution)/shard_map/psum | solution.py:471
  13.7 11.1 %collective-permute-start.1 = (bf16[128,1024]{1,0:T(8,128)(2,1)S(1)}, bf16[128,1024]{1,0:T(8,128)(2,1)S(1)}, u32[]{:S(2)}, u32[]{:S(2)}) collective-permute-start(bf16[128,1024]{1,0:T(8,128)(2,1)S(1)} %fusion.5), channel_id=1, source_target_pairs={{0,8},{8,16},{16,24},{24,32},{32,40},{40,48},{48,56},{56,64},{64,7... | collective-permute-start | bytes 786440 | tf_op jit(solution)/shard_map/ppermute | solution.py:431
  18.1 6.7 %collective-permute-start = (bf16[3,16,1024]{2,1,0:T(8,128)(2,1)S(1)}, bf16[3,16,1024]{2,1,0:T(8,128)(2,1)S(1)}, u32[]{:S(2)}, u32[]{:S(2)}) collective-permute-start(bf16[3,16,1024]{2,1,0:T(8,128)(2,1)S(1)} %slice.54), channel_id=1, source_target_pairs={{0,8},{8,16},{16,24},{24,32},{32,40},{40,48},{48,56},{56,64},{64,7... | collective-permute-start | bytes 294920 | tf_op jit(solution)/shard_map/ppermute | solution.py:431
  24.8 0.6 copy-start.4
  24.8 0.7 copy-start.2
  151.0 10.4 %copy-start = (bf16[256,1024]{1,0:T(8,128)(2,1)}, bf16[256,1024]{1,0:T(8,128)(2,1)S(1)}, u32[]{:S(2)}) copy-start(bf16[256,1024]{1,0:T(8,128)(2,1)S(1)} %convolution_convert_fusion.1.gg_ref) | copy-start | bytes 1572868
  152.3 9.1 %collective-permute-start.2 = (bf16[128,1024]{1,0:T(8,128)(2,1)S(1)}, bf16[128,1024]{1,0:T(8,128)(2,1)S(1)}, u32[]{:S(2)}, u32[]{:S(2)}) collective-permute-start(bf16[128,1024]{1,0:T(8,128)(2,1)S(1)} %fusion.1), channel_id=1, source_target_pairs={{8,0},{16,8},{24,16},{32,24},{40,32},{48,40},{56,48},{64,56},{72,6... | collective-permute-start | bytes 786440 | tf_op jit(solution)/shard_map/ppermute | solution.py:431
  161.4 0.7 copy-start.1
  198.9 6.5 %collective-permute-start.3 = (f32[3,8,8,128]{3,2,1,0:T(8,128)S(1)}, f32[3,8,8,128]{3,2,1,0:T(8,128)S(1)}, u32[]{:S(2)}, u32[]{:S(2)}) collective-permute-start(f32[3,8,8,128]{3,2,1,0:T(8,128)S(1)} %slice.69), channel_id=1, source_target_pairs={{8,0},{16,8},{24,16},{32,24},{40,32},{48,40},{56,48},{64,56},{72,6... | collective-permute-start | bytes 294920 | tf_op jit(solution)/shard_map/ppermute | solution.py:431
  205.4 0.6 copy-start.3
  206.0 8.3 %copy-start.5 = (bf16[256,1024]{1,0:T(8,128)(2,1)S(1)}, bf16[256,1024]{1,0:T(8,128)(2,1)}, u32[]{:S(2)}) copy-start(bf16[256,1024]{1,0:T(8,128)(2,1)} %get-tuple-element.17) | copy-start | bytes 1572868
  214.3 124.2 %reduce-scatter.2.cloned.1.call-start = ((), (), s32[]{:S(2)}) async-start(), calls=%async_computation.2 | async-start | bytes 3538944 | tf_op jit(solution)/shard_map/reduce_scatter | solution.py:463
Sparse Core Ops, SparseCore 0:
  9.7 30.2 all-gather.4
  42.1 99.8 all-gather.2
  214.4 86.8 all-reduce.2
  304.1 34.3 reduce-scatter.1

commit v2 on v1

--- a/solution.py
+++ b/solution.py
@@ -1,6 +1,3 @@
-import functools
-import math
-
 import jax
 import jax.numpy as jnp
 import numpy as np
@@ -73,11 +70,10 @@
     return lax.rem(lax.broadcasted_iota(jnp.int32, (count, 128), 0), BLK)
 
 
-def load_inputs(proj_ref, jhalo_ref, pj):
+def load_inputs(source, pj, first, count):
     def lane(l, carry):
         for b in range(3):
-            pj[b, l, 0:PAD, :] = jhalo_ref[b, :, lanes(l)].astype(F32)
-            pj[b, l, PAD : PAD + ROWS, :] = proj_ref[b, :, lanes(l)].astype(F32)
+            pj[b, l, first : first + count, :] = source[b, :, lanes(l)].astype(F32)
         return carry
 
     lax.fori_loop(0, LB, lane, 0)
@@ -101,8 +97,8 @@
         xs[l, rows_at(PAD + r0, 64), :] = wide
         live = room_ref[rows_at(128 + r0, 64), :] >= BLK - inside
         xv[pl.ds(pl.multiple_of(128 + r0, 16), 64), lanes(l)] = jnp.where(live, wide, 0.0).astype(BF16)
-        if prod is not None:
-            prod[pl.ds(pl.multiple_of(r0, 16), 64), lanes(l)] = product
+        if first:
+            prod[pl.ds(pl.multiple_of(r0 - 128, 16), 64), lanes(l)] = product
         return carry
 
     lax.fori_loop(0, LB * count, step, 0)
@@ -250,11 +246,14 @@
     lax.fori_loop(0, LB * 4, step, 0)
 
 
-def make_long(gg_ref, feats, age_ref, gs_, gv, first, count):
+def make_long(gg_ref, feats, age_ref, gs_, gl, gv, first, count):
     def step(at, carry):
         l, r0 = at // count, (first + at % count) * 64
         rows = pl.ds(pl.multiple_of(r0, 16), 64)
-        long = (gg_ref[rows, lanes(l)].astype(F32) * feats[0, l, rows_at(r0, 64), :]).astype(BF16).astype(F32)
+        sent = (gg_ref[rows, lanes(l)].astype(F32) * feats[0, l, rows_at(r0, 64), :]).astype(BF16)
+        long = sent.astype(F32)
+        if not first:
+            gl[rows, lanes(l)] = sent
         gs_[l, rows_at(r0, 64), :] = long
         live = age_ref[rows_at(128 + r0, 64), :] > in_block(64)
         gv[rows, lanes(l)] = jnp.where(live, long, 0.0).astype(BF16)
@@ -306,170 +305,371 @@
     lax.fori_loop(0, LB, lane, 0)
 
 
-def last_step(gf, pj, fw_ref, age_ref, room_ref, gproj_ref, short_ref):
+def short_sums(gf, pj, age_ref, short):
     def lane(l, carry):
         def step(i, sums):
             r0 = i * 64
             age = age_ref[rows_at(128 + r0, 64), :]
-            room = room_ref[rows_at(128 + r0, 64), :]
             out = []
             for b in range(3):
                 here = gf[b, l, rows_at(r0, 64), :]
-                total = here * fw_ref[b, 0:1, lanes(l)]
-                for i_tap in range(3):
-                    window = pj[b, l, pl.ds(PAD + r0 - i_tap, 64), :]
-                    if i_tap:
-                        later = gf[b, l, pl.ds(r0 + i_tap, 64), :]
-                        total = total + jnp.where(room > i_tap, later, 0.0) * fw_ref[b, i_tap : i_tap + 1, lanes(l)]
-                        window = jnp.where(age >= i_tap, window, 0.0)
-                    out.append(sums[b * 3 + i_tap] + jnp.sum((here * window).reshape(8, 8, 128), axis=0))
-                gproj_ref[b, pl.ds(pl.multiple_of(r0, 16), 64), lanes(l)] = total.astype(BF16)
+                for tap in range(3):
+                    window = pj[b, l, pl.ds(PAD + r0 - tap, 64), :]
+                    if tap:
+                        window = jnp.where(age >= tap, window, 0.0)
+                    out.append(sums[b * 3 + tap] + jnp.sum((here * window).reshape(8, 8, 128), axis=0))
             return tuple(out)
 
         sums = lax.fori_loop(0, 4, step, (jnp.zeros((8, 128), F32),) * 9)
         for at in range(9):
-            short_ref[at : at + 1, lanes(l)] = jnp.sum(sums[at], axis=0, keepdims=True)
+            short[at : at + 1, lanes(l)] = jnp.sum(sums[at], axis=0, keepdims=True)
         return carry
 
     lax.fori_loop(0, LB, lane, 0)
 
 
-def kernel_forward(
-    base_ref, seg_ref, proj_ref, jhalo_ref, phalo_ref, fw_ref, lf_ref, tab_ref, tabt_ref,
-    gated, feats, filt, spec_x, spec_g, xs, pj, age_ref, room_ref, xv, spec_y, wide, lfb,
+def input_grads(gf, fw_ref, room_ref, gproj_ref):
+    def step(at, carry):
+        l, r0 = at // 4, (at % 4) * 64
+        room = room_ref[rows_at(128 + r0, 64), :]
+        for b in range(3):
+            total = gf[b, l, rows_at(r0, 64), :] * fw_ref[b, 0:1, lanes(l)]
+            for tap in range(1, 3):
+                later = gf[b, l, pl.ds(r0 + tap, 64), :]
+                total = total + jnp.where(room > tap, later, 0.0) * fw_ref[b, tap : tap + 1, lanes(l)]
+            gproj_ref[b, pl.ds(pl.multiple_of(r0, 16), 64), lanes(l)] = total.astype(BF16)
+        return carry
+
+    lax.fori_loop(0, LB * 4, step, 0)
+
+
+MESH = pl.DeviceIdType.MESH
+NX = 4
+COLS = 384
+WIDE = NX * COLS
+OWN = 32
+PEERS = 16
+
+
+def turned(at, by):
+    return lax.rem(at + by + 2 * NX, NX)
+
+
+def kernel(
+    seg_ref, proj_ref, fw_ref, lf_ref, w_ref, cot_ref, tab_ref, tabt_ref,
+    out_ref, gproj_ref, taps_ref, short_ref,
+    pj, feats, filt, xs, xv, prod, jhalo, phalo, age_ref, room_ref, lfb, spec_x, spec_g, spec_y, wide,
+    gs_, gl, gv, glhalo, spec_z, spec_q, gf, gfhalo, taps, near_taps, short,
+    wg, cg, ga_own, ga_back, ga_fore, ga_far, part_own, part_back, part_fore, part_far, rs_a, rs_b, rs_c, rs_t, gg,
+    ob_own, ob_back, ob_fore, ob_far, co_own, co_back, co_fore, co_far, sb, y_a, y_b, y_c, y_t, rb, fin, pk, rk, tot, fk,
+    send, recv, t_send, t_recv, u_send, u_recv,
 ):
-    find_ages(seg_ref, base_ref[0], age_ref, room_ref)
-    load_inputs(proj_ref, jhalo_ref, pj)
+    ctx, tp = lax.axis_index("ctx"), lax.axis_index("tp")
+    z, x, y, core = ctx // 4, ctx % 4, tp // 2, tp % 2
+    way = 1 - 2 * core
+    other = (ctx, y * 2 + (1 - core))
+
+    def at_x(by):
+        return (z * 4 + turned(x, by), tp)
+
+    def at_z(by):
+        return (turned(z, by) * 4 + x, tp)
+
+    def at_y(by):
+        return (ctx, turned(y, by) * 2 + core)
+
+    def at_ctx(by):
+        return (lax.rem(ctx + by + PEERS, PEERS), tp)
+
+    barrier = pltpu.get_barrier_semaphore()
+    for by in range(1, PEERS):
+        pl.semaphore_signal(barrier, inc=1, device_id=at_ctx(by), device_id_type=MESH)
+    for peer in (at_y(1), at_y(-1), other):
+        pl.semaphore_signal(barrier, inc=1, device_id=peer, device_id_type=MESH)
+    pl.semaphore_wait(barrier, PEERS + 2)
+
+    started = []
+
+    def remote(slot, source, target, peer):
+        copy = pltpu.make_async_remote_copy(
+            src_ref=source, dst_ref=target, send_sem=send.at[slot], recv_sem=recv.at[slot],
+            device_id=peer, device_id_type=MESH,
+        )
+        copy.start()
+        started.append(copy)
+        return copy
+
+    w_ahead = remote(0, w_ref, wg.at[x], at_x(way))
+    w_behind = remote(1, w_ref, wg.at[x], at_x(-way))
+    cot_in = []
+    for by in range(1, 4):
+        cols = pl.ds(pl.multiple_of(turned(z, by) * WIDE, 128), WIDE)
+        cot_in.append(remote(2 + by, cot_ref.at[:, cols], cg.at[tp, z], at_z(by)))
+    j_copy = remote(13, proj_ref.at[:, pl.ds(ROWS - 16, 16), :], jhalo, at_ctx(1))
+    wg[x] = w_ref[...]
+    cg[tp, z] = cot_ref[:, pl.ds(pl.multiple_of(z * WIDE, 128), WIDE)]
+
+    find_ages(seg_ref, ctx * ROWS, age_ref, room_ref)
+    load_inputs(proj_ref, pj, PAD, ROWS)
     xs[:, 0:PAD, :] = jnp.zeros((LB, PAD, 128), F32)
-    features(pj, fw_ref, age_ref, room_ref, feats, xs, xv, None, 0, 4)
-    mask_halo(phalo_ref, room_ref, xv)
+    features(pj, fw_ref, age_ref, room_ref, feats, xs, xv, prod, 2, 2)
+    p_copy = remote(14, prod, phalo, at_ctx(1))
+
+    def slab(by):
+        return cg.at[turned(y, by) * 2 + core]
+
+    for copy in cot_in:
+        copy.wait_recv()
+    cot_ahead = remote(6, slab(0), slab(0), at_y(way))
+    cot_behind = remote(7, slab(0), slab(0), at_y(-way))
+    cot_core = [remote(9, slab(0), slab(0), other)]
+
+    j_copy.wait_recv()
+    load_inputs(jhalo, pj, 0, PAD)
+    features(pj, fw_ref, age_ref, room_ref, feats, xs, xv, prod, 0, 2)
     lfb[...] = lf_ref[...].astype(BF16)
     transform(tab_ref[2], lfb, spec_g, 0)
-    for group in range(3):
+    for group in (1, 2):
         transform(tab_ref[0], xv, spec_x, group)
+
+    p_copy.wait_recv()
+    mask_halo(phalo, room_ref, xv)
+    transform(tab_ref[0], xv, spec_x, 0)
+    cot_ahead.wait_recv()
+    cot_on = remote(8, slab(-way), slab(-way), at_y(way))
+    cot_core.append(remote(10, slab(-way), slab(-way), other))
+    cot_behind.wait_recv()
+    cot_core.append(remote(11, slab(way), slab(way), other))
     far_forward(spec_x, spec_g, age_ref, spec_y)
     inverse(tabt_ref[1], spec_y, wide, 2)
-    near_forward(xs, lf_ref, age_ref, wide, feats, filt, gated)
-
-
-def kernel_back(
-    gg_ref, glhalo_ref, lf_ref, tab_ref, tabt_ref, feats, filt, spec_x, spec_g, xs, age_ref, room_ref,
-    gf, taps_ref, gs_, gv, spec_z, spec_p, spec_q, wide, near_taps,
-):
-    make_long(gg_ref, feats, age_ref, gs_, gv, 0, 4)
+    w_ahead.wait_recv()
+    w_on = remote(2, wg.at[turned(x, -way)], wg.at[turned(x, -way)], at_x(way))
+    near_forward(xs, lf_ref, age_ref, wide, feats, filt, ga_own)
+    ga_ahead = remote(15, ga_own, ga_back, at_z(way))
+    ga_behind = remote(16, ga_own, ga_fore, at_z(-way))
+
+    cot_on.wait_recv()
+    cot_core.append(remote(12, slab(2), slab(2), other))
+    for copy in cot_core:
+        copy.wait_recv()
+    w_behind.wait_recv()
+    w_on.wait_recv()
+
+    def backward_part(block, target):
+        def step(n, carry):
+            rows = pl.ds(pl.multiple_of(n * 256, 256), 256)
+            total = jnp.zeros((ROWS, 256), F32)
+            for at in range(NX):
+                total = total + lax.dot_general(
+                    cg[:, block, :, at * COLS : (at + 1) * COLS].reshape(ROWS, COLS), wg[at, rows, :],
+                    (((1,), (1,)), ((), ())), preferred_element_type=F32,
+                )
+            target[:, rows] = total.astype(BF16)
+            return carry
+
+        lax.fori_loop(0, CH // 256, step, 0)
+
+    backward_part(turned(z, 2), part_far)
+    s_a = remote(18, part_far, rs_a, at_z(way))
+    backward_part(turned(z, -way), part_back)
+    s_b = remote(19, part_back, rs_b, at_z(-way))
+    ga_ahead.wait_recv()
+    ga_on = remote(17, ga_back, ga_far, at_z(way))
+    backward_part(turned(z, way), part_fore)
+    backward_part(z, part_own)
+
+    def forward_part(rows, target):
+        def step(at, carry):
+            got = jnp.dot(rows[...], wg[at], preferred_element_type=F32)
+            cols = pl.ds(pl.multiple_of(at * COLS, 128), COLS)
+            target[:, :, :, cols] = got.astype(BF16).reshape(4, 2, OWN, COLS)
+            return carry
+
+        lax.fori_loop(0, NX, step, 0)
+
+    forward_part(ga_own, ob_own)
+    o_core = [remote(21, ob_own.at[:, 1 - core], co_own, other)]
+
+    s_a.wait_recv()
+
+    def add_rows(target, terms, count):
+        def step(i, carry):
+            rows = pl.ds(pl.multiple_of(i * 64, 64), 64)
+            total = terms[0][rows, :].astype(F32)
+            for term in terms[1:]:
+                total = total + term[rows, :].astype(F32)
+            target[rows, :] = total.astype(BF16)
+            return carry
+
+        lax.fori_loop(0, count // 64, step, 0)
+
+    add_rows(rs_t, (rs_a, part_fore), ROWS)
+    s_c = remote(20, rs_t, rs_c, at_z(way))
+
+    forward_part(ga_back, ob_back)
+    o_core.append(remote(22, ob_back.at[:, 1 - core], co_fore, other))
+    ga_behind.wait_recv()
+    forward_part(ga_fore, ob_fore)
+    o_core.append(remote(23, ob_fore.at[:, 1 - core], co_back, other))
+    ga_on.wait_recv()
+    forward_part(ga_far, ob_far)
+    o_core.append(remote(24, ob_far.at[:, 1 - core], co_far, other))
+
+    s_b.wait_recv()
+    s_c.wait_recv()
+    add_rows(gg, (part_own, rs_b, rs_c), ROWS)
+    make_long(gg, feats, age_ref, gs_, gl, gv, 0, 2)
+    l_copy = remote(31, gl, glhalo, at_ctx(-1))
+
+    for copy in o_core:
+        copy.wait_recv()
+
+    def add_core(q, carry):
+        blocks = ((0, ob_own, co_own), (-way, ob_back, co_back), (way, ob_fore, co_fore), (2, ob_far, co_far))
+        for by, mine, theirs in blocks:
+            sb[q, turned(z, by)] = (mine[q, core].astype(F32) + theirs[q].astype(F32)).astype(BF16)
+        return carry
+
+    lax.fori_loop(0, 4, add_core, 0)
+    y_1 = remote(25, sb.at[turned(y, 2)], y_a, at_y(way))
+    y_2 = remote(26, sb.at[turned(y, -way)], y_b, at_y(-way))
+
+    make_long(gg, feats, age_ref, gs_, gl, gv, 2, 2)
     gs_[:, ROWS : ROWS + PAD, :] = jnp.zeros((LB, PAD, 128), F32)
-    mask_next(glhalo_ref, age_ref, gv)
-    for group in range(3):
+    for group in (0, 1):
         transform(tab_ref[1], gv, spec_z, group)
-    far_back(spec_z, spec_g, age_ref, spec_p)
-    inverse(tabt_ref[0], spec_p, wide, 2)
     far_taps(spec_x, spec_z, age_ref, spec_q)
-    near_back(gs_, xs, lf_ref, age_ref, room_ref, wide, gg_ref, filt, feats, gf, near_taps)
-    inverse(tabt_ref[2], spec_q, taps_ref, 1)
-    taps_ref[0:BLK, :] = taps_ref[0:BLK, :] + near_taps[...]
-
-
-def kernel_last(gf_ref, gfhalo_ref, pj, fw_ref, age_ref, room_ref, gproj_ref, short_ref, gf):
-    gf[:, :, 0:ROWS, :] = gf_ref[...]
-    gf[:, :, ROWS : ROWS + 8, :] = gfhalo_ref[...]
-    last_step(gf, pj, fw_ref, age_ref, room_ref, gproj_ref, short_ref)
-
-
-def call(kernel, outs, scratch, smem, args):
+
+    y_1.wait_recv()
+
+    def add_blocks(target, terms):
+        for zz in range(4):
+            total = terms[0][zz].astype(F32)
+            for term in terms[1:]:
+                total = total + term[zz].astype(F32)
+            target[zz] = total.astype(BF16)
+
+    add_blocks(y_t, (y_a, sb.at[turned(y, way)]))
+    y_3 = remote(27, y_t, y_c, at_y(way))
+
+    l_copy.wait_recv()
+    mask_next(glhalo, age_ref, gv)
+    transform(tab_ref[1], gv, spec_z, 2)
+    far_back(spec_z, spec_g, age_ref, spec_y)
+    inverse(tabt_ref[0], spec_y, wide, 2)
+    near_back(gs_, xs, lf_ref, age_ref, room_ref, wide, gg, filt, feats, gf, near_taps)
+    f_copy = remote(32, gf.at[:, :, pl.ds(0, 8), :], gfhalo, at_ctx(-1))
+
+    y_2.wait_recv()
+    y_3.wait_recv()
+    add_blocks(rb, (sb.at[y], y_b, y_c))
+    outs = [remote(27 + by, rb.at[turned(z, by)], fin.at[z], at_z(by)) for by in range(1, 4)]
+
+    inverse(tabt_ref[2], spec_q, taps, 1)
+    taps[0:BLK, :] = taps[0:BLK, :] + near_taps[...]
+    short_sums(gf, pj, age_ref, short)
+    for q in range(PEERS):
+        rows = taps[q * 8 : (q + 1) * 8, :]
+        pk[q, :, 0:512] = jnp.concatenate([rows[:, 0:512], rows[:, 512:1024]], axis=0).astype(BF16)
+        if q < 9:
+            row = [short[q : q + 1, i * 128 : (i + 1) * 128] for i in range(8)]
+            row.append(jnp.zeros((8, 128), F32))
+            pk[q, :, 512:640] = jnp.concatenate(row, axis=0).astype(BF16)
+        else:
+            pk[q, :, 512:640] = jnp.zeros((16, 128), BF16)
+
+    def tap_copy(i):
+        peer = lax.rem(ctx + i, PEERS)
+        return pltpu.make_async_remote_copy(
+            src_ref=pk.at[peer], dst_ref=rk.at[i], send_sem=t_send.at[i], recv_sem=t_recv.at[i],
+            device_id=(peer, tp), device_id_type=MESH,
+        )
+
+    def total_copy(i):
+        peer = lax.rem(ctx + i, PEERS)
+        return pltpu.make_async_remote_copy(
+            src_ref=tot, dst_ref=fk.at[ctx], send_sem=u_send.at[i], recv_sem=u_recv.at[i],
+            device_id=(peer, tp), device_id_type=MESH,
+        )
+
+    def each(make, act):
+        def step(i, carry):
+            act(make(i))
+            return carry
+
+        lax.fori_loop(1, PEERS, step, 0)
+
+    each(tap_copy, lambda copy: copy.start())
+    f_copy.wait_recv()
+    gf[:, :, ROWS : ROWS + 8, :] = gfhalo[...]
+    input_grads(gf, fw_ref, room_ref, gproj_ref)
+
+    for copy in outs:
+        copy.wait_recv()
+    out_ref[:, pl.ds(pl.multiple_of(z * WIDE, 128), WIDE)] = rb[z]
+    for by in range(1, 4):
+        block = turned(z, by)
+        out_ref[:, pl.ds(pl.multiple_of(block * WIDE, 128), WIDE)] = fin[block]
+
+    each(tap_copy, lambda copy: copy.wait_recv())
+    total = pk[ctx].astype(F32)
+    for i in range(1, PEERS):
+        total = total + rk[i].astype(F32)
+    tot[...] = total.astype(BF16)
+    fk[ctx] = tot[...]
+    each(total_copy, lambda copy: copy.start())
+    each(total_copy, lambda copy: copy.wait_recv())
+    norm = TOKENS**-0.5
+    for q in range(PEERS):
+        done = fk[q].astype(F32) * norm
+        taps_ref[q * 8 : (q + 1) * 8, 0:512] = done[0:8, 0:512]
+        taps_ref[q * 8 : (q + 1) * 8, 512:1024] = done[8:16, 0:512]
+        if q < 9:
+            for i in range(8):
+                short_ref[q // 3, q % 3 : q % 3 + 1, i * 128 : (i + 1) * 128] = done[i : i + 1, 512:640]
+
+    each(tap_copy, lambda copy: copy.wait_send())
+    each(total_copy, lambda copy: copy.wait_send())
+    for copy in started:
+        copy.wait_send()
+
+
+def shards(projected, feat_weight, long_filter, out_weight, seg_lengths, cotangent):
+    tab, tabt = (jnp.asarray(t) for t in tables())
     vm = pl.BlockSpec(memory_space=pltpu.VMEM)
-    sm = pl.BlockSpec(memory_space=pltpu.SMEM)
+    laned = (LB, ROWS, 128)
+    padded = (LB, PAD + ROWS, 128)
+    spec = (3 * 256, CH)
+    age = (512, 128)
+    block = (4, OWN, WIDE)
+    scratch = [
+        ((3,) + padded, F32), ((3,) + laned, F32), (laned, F32), (padded, F32), ((128 + ROWS, CH), BF16),
+        ((128, CH), BF16), ((3, 16, CH), BF16), ((128, CH), BF16), (age, jnp.int32), (age, jnp.int32),
+        ((128, CH), BF16), (spec, F32), ((256, CH), F32), ((512, CH), F32), ((ROWS, CH), F32),
+        (padded, F32), ((128, CH), BF16), ((ROWS + 128, CH), BF16), ((128, CH), BF16), (spec, F32), ((256, CH), F32),
+        ((3,) + padded, F32), ((3, LB, 8, 128), F32), ((128, CH), F32), ((BLK, CH), F32), ((16, CH), F32),
+        ((NX, CH, COLS), BF16), ((8,) + block, BF16),
+        *[((ROWS, CH), BF16)] * 13, *[((4, 2, OWN, WIDE), BF16)] * 4, *[(block, BF16)] * 4, ((4,) + block, BF16),
+        (block, BF16), (block, BF16), (block, BF16), (block, BF16), (block, BF16), (block, BF16),
+        ((PEERS, 16, 640), BF16), ((PEERS, 16, 640), BF16), ((16, 640), BF16), ((PEERS, 16, 640), BF16),
+    ]
+    dma = pltpu.SemaphoreType.DMA
     return pl.pallas_call(
         kernel,
-        out_shape=[jax.ShapeDtypeStruct(s, d) for s, d in outs],
-        in_specs=[sm] * smem + [vm] * (len(args) - smem),
-        out_specs=[vm] * len(outs),
-        scratch_shapes=[pltpu.VMEM(s, d) for s, d in scratch],
-        compiler_params=pltpu.CompilerParams(vmem_limit_bytes=56 * 2**20),
-    )(*args)
-
-
-SPEC = ((3 * 256, CH), F32)
-AGE = ((512, 128), jnp.int32)
-LANED = ((LB, ROWS, 128), F32)
-
-
-def forward_call(base, seg, proj, jhalo, phalo, fw, lf, tab, tabt):
-    return call(
-        kernel_forward,
-        [((ROWS, CH), BF16), ((3,) + LANED[0], F32), LANED, SPEC, ((256, CH), F32),
-         ((LB, PAD + ROWS, 128), F32), ((3, LB, PAD + ROWS, 128), F32), AGE, AGE],
-        [((128 + ROWS, CH), BF16), ((512, CH), F32), ((ROWS, CH), F32), ((128, CH), BF16)],
-        2,
-        (base, seg, proj, jhalo, phalo, fw, lf, tab, tabt),
-    )
-
-
-def back_call(*args):
-    return call(
-        kernel_back,
-        [((3,) + LANED[0], F32), ((128, CH), F32)],
-        [((LB, ROWS + PAD, 128), F32), ((ROWS + 128, CH), BF16), SPEC, ((512, CH), F32), ((256, CH), F32),
-         ((ROWS, CH), F32), ((BLK, CH), F32)],
-        0,
-        args,
-    )
-
-
-def last_call(*args):
-    return call(
-        kernel_last,
-        [((3, ROWS, CH), BF16), ((9, CH), F32)],
-        [((3, LB, ROWS + PAD, 128), F32)],
-        0,
-        args,
-    )
-
-
-def from_behind(x, axis, by):
-    size = lax.axis_size(axis)
-    pairs = [(i, i + by) for i in range(size) if 0 <= i + by < size]
-    return lax.ppermute(x, axis, pairs)
-
-
-def segment_ages(positions, seg_lengths):
-    seg_starts = jnp.cumsum(seg_lengths) - seg_lengths
-    earlier = jnp.where(seg_starts[None, :] <= positions[:, None], seg_starts[None, :], 0)
-    return positions - jnp.max(earlier, axis=1)
-
-
-def shards(projected, feat_weight, long_filter, out_weight, seg_lengths, cotangent):
-    tab, tabt = (jnp.asarray(t) for t in tables())
-    base = lax.axis_index("ctx") * ROWS
-    cot_rows = lax.all_gather(cotangent, "tp", axis=0, tiled=True)
-    weight = lax.all_gather(out_weight, "ctx", axis=1, tiled=True)
-    jhalo = from_behind(projected[:, ROWS - 16 :, :], "ctx", 1)
-    tail_age = segment_ages(base + 128 + jnp.arange(128, dtype=jnp.int32), seg_lengths)
-    tail = []
-    for b in (1, 2):
-        total = 0.0
-        for i in range(3):
-            window = projected[b, 128 - i : 256 - i].astype(F32)
-            total = total + jnp.where((tail_age >= i)[:, None], window * feat_weight[b, i][None, :], 0.0)
-        tail.append(total)
-    phalo = from_behind((tail[0] * tail[1]).astype(BF16), "ctx", 1)
-    gated, feats, filt, spec_x, spec_g, xs, pj, age, room = forward_call(
-        base.reshape(1), seg_lengths, projected, jhalo, phalo, feat_weight, long_filter, tab, tabt
-    )
-    grad_gated = lax.dot_general(cot_rows, weight, (((1,), (1,)), ((), ())), preferred_element_type=F32)
-    grad_gated = grad_gated.astype(BF16)
-    front = jnp.swapaxes(feats[0, :, :128, :], 0, 1).reshape(128, CH)
-    glhalo = from_behind((grad_gated[:128] * front).astype(BF16), "ctx", -1)
-    terms = jnp.dot(gated, weight, preferred_element_type=F32)
-    summed = lax.psum_scatter(terms.astype(BF16), "tp", scatter_dimension=0, tiled=True)
-    gf, taps = back_call(
-        grad_gated, glhalo, long_filter, tab, tabt, feats, filt, spec_x, spec_g, xs, age, room
-    )
-    gfhalo = from_behind(gf[:, :, :8, :], "ctx", -1)
-    grad_inputs, short = last_call(gf, gfhalo, pj, feat_weight, age, room)
-    norm = TOKENS**-0.5
-    both = jnp.concatenate([taps, jnp.pad(short, ((0, 7), (0, 0)))], axis=0).astype(BF16)
-    both = lax.psum(both, "ctx").astype(F32) * norm
-    return (summed, grad_inputs, both[:128], both[128:137].reshape(3, 3, CH))
+        out_shape=[
+            jax.ShapeDtypeStruct((OWN, 4 * WIDE), BF16),
+            jax.ShapeDtypeStruct((3, ROWS, CH), BF16),
+            jax.ShapeDtypeStruct((128, CH), F32),
+            jax.ShapeDtypeStruct((3, 3, CH), F32),
+        ],
+        in_specs=[pl.BlockSpec(memory_space=pltpu.SMEM)] + [vm] * 7,
+        out_specs=[vm] * 4,
+        scratch_shapes=[pltpu.VMEM(s, d) for s, d in scratch]
+        + [dma((33,)), dma((33,)), dma((PEERS,)), dma((PEERS,)), dma((PEERS,)), dma((PEERS,))],
+        compiler_params=pltpu.CompilerParams(
+            collective_id=0, has_side_effects=True, vmem_limit_bytes=60 * 2**20
+        ),
+    )(seg_lengths, projected, feat_weight, long_filter, out_weight, cotangent, tab, tabt)
 
 
 def solution(mesh):

time: 346 us -> 144 us (0.42)
  waiting for transfers between devices: 219 us -> 0 us
  Pallas kernels: 69.3 us -> 137 us
  matrix products: 18.3 us -> 0 us
  between operations: 13.9 us -> 0.64 us
  starting transfers between devices: 9.6 us -> 0 us
  other arithmetic: 8.29 us -> 0 us
    all_gather x2 -> x0, waiting for transfers between devices: 89.7 us -> none  [the longest x1 89.7 us: shards(): weight = lax.all_gather(out_weight, 'ctx', axis=1, tiled=True)]
    psum x1 -> x0, waiting for transfers between devices: 77.6 us -> none  [shards(): both = lax.psum(both, 'ctx').astype(F32) * norm]
    pallas_call x3 -> x1, Pallas kernels: 69.3 us -> 137 us  [shards(): pl.pallas_call(kernel, out_shape=[jax.ShapeDtypeStruct((OWN, 4 * WIDE), B...]
    reduce_scatter x1 -> x0, waiting for transfers between devices: 34.7 us -> none  [shards(): lax.psum_scatter(terms.astype(BF16), 'tp', scatter_dimension=0, tiled=True)]
    dot_general x2 -> x0, matrix products: 18.3 us -> none  [the longest x1 9.37 us: shards(): terms = jnp.dot(gated, weight, preferred_element_type=F32)]
    ppermute x4 -> x0, waiting for transfers between devices: 15.3 us -> none  [from_behind(): return lax.ppermute(x, axis, pairs)]
    ppermute x4 -> x0, starting transfers between devices: 9.44 us -> none  [from_behind(): return lax.ppermute(x, axis, pairs)]
    unnamed x12 -> x8, local copies, waits for them, and re-layouts: 2.08 us -> 5.91 us
  transfers between devices with their start and end apart: 8 -> 0, of which waited for: 6 -> 0; matrix products, arithmetic and copies ran while one was open for 5% -> 0% of each run, Pallas kernels for 8% -> 0%
where the time goes in v2:
time: 144 us; the launch traced here: 143 us
  Pallas kernels  137 us (95%)
  local copies, waits for them, and re-layouts  5.91 us (4%)
    pallas_call x1, Pallas kernels, shards(): pl.pallas_call(kernel, out_shape=[jax.ShapeDtypeStruct((OWN, 4 * WIDE), B...  137 us
    unnamed x8, local copies, waits for them, and re-layouts  5.91 us

profile of v2, /device:TPU:0, one launch (start us, length us, event | category | flops | bytes accessed | tf_op | source)
XLA Modules:
  0.0 143.2 jit_solution(5708858227633638628)
XLA Ops:
  0.6 136.6 %shard_map.111 = (bf16[32,6144]{1,0:T(8,128)(2,1)}, bf16[3,256,1024]{2,1,0:T(8,128)(2,1)}, f32[128,1024]{1,0:T(8,128)}, f32[3,3,1024]{2,1,0:T(4,128)}) custom-call(s32[32]{0:T(128)} %seg_ref.1, bf16[3,256,1024]{2,1,0:T(8,128)(2,1)} %proj_ref.1, f32[3,3,1024]{2,1,0:T(4,128)} %fw_ref.1, f32[128,1024]{1,0:T(8,128)} %lf_ref.1, bf16[1024,384]{1,0:T(8,128)(2,1)} %w_ref.1, ...), custom_call_target="tpu_custom_call" | custom-call | tf_op jit(solution)/shard_map/pallas_call | solution.py:657
  137.2 1.8 %copy.16 = bf16[32,6144]{1,0:T(8,128)(2,1)} copy(bf16[32,6144]{1,0:T(8,128)(2,1)} %get-tuple-element.8) | data formatting | bytes 786432
  139.0 0.0 copy-start
  139.0 0.0 copy-start.1
  139.0 2.7 %copy.17 = bf16[3,256,1024]{2,1,0:T(8,128)(2,1)} copy(bf16[3,256,1024]{2,1,0:T(8,128)(2,1)} %get-tuple-element.9) | data formatting | bytes 3145728
  141.7 0.0 copy-done
  141.7 0.8 copy.18
  142.5 0.0 copy-done.1
  142.5 0.6 copy.19
Async XLA Ops:
  139.0 2.7 %copy-start = (f32[128,1024]{1,0:T(8,128)S(1)}, f32[128,1024]{1,0:T(8,128)}, u32[]{:S(2)}) copy-start(f32[128,1024]{1,0:T(8,128)} %get-tuple-element.10) | copy-start | bytes 1572868
  139.0 3.5 %copy-start.1 = (f32[3,3,1024]{2,1,0:T(4,128)S(1)}, f32[3,3,1024]{2,1,0:T(4,128)}, u32[]{:S(2)}) copy-start(f32[3,3,1024]{2,1,0:T(4,128)} %get-tuple-element.11) | copy-start | bytes 110596

commit v3 on v2

v3 whole, which is shorter than its diff:
```python
import jax
import jax.numpy as jnp
import numpy as np
from jax import lax
from jax.experimental import pallas as pl
from jax.experimental.pallas import tpu as pltpu
from jax.sharding import PartitionSpec as P

F32 = jnp.float32
BF16 = jnp.bfloat16
ROWS = 256
CH = 1024
LB = CH // 128
BLK = 16
FAR = 8
TOKENS = 4096
NSEG = 32
PAD = 16
CHUNKS = 4
SPAN = LB // CHUNKS


def tables():
    turn = np.pi * (2 * np.arange(BLK) + 1) / (2 * BLK)

    def wave(at):
        return np.concatenate([np.cos(np.outer(turn, at)), -np.sin(np.outer(turn, at))])

    into = wave(np.arange(BLK))
    back = wave(np.arange(BLK) + BLK) / BLK
    back[BLK:] = -back[BLK:]
    taps = np.zeros((FAR * 2 * BLK, FAR * BLK))
    window = wave(np.arange(2 * BLK))
    for k in range(FAR):
        for d in range(1, 2 * BLK):
            if k * BLK + d < FAR * BLK:
                taps[k * 2 * BLK : (k + 1) * 2 * BLK, k * BLK + d] = window[:, d]
    each = np.eye(FAR)
    stack = np.stack([np.kron(each, into), np.kron(each, back), taps])
    return stack.astype(jnp.bfloat16), np.swapaxes(stack, 1, 2).astype(jnp.bfloat16)


def lanes(l):
    return pl.ds(pl.multiple_of(l * 128, 128), 128)


def rows_at(start, count):
    return pl.ds(pl.multiple_of(start, 8), count)


def find_ages(seg_ref, base, age_ref, room_ref):
    def chunk(i, carry):
        at = rows_at(i * 64, 64)
        pos = lax.broadcasted_iota(jnp.int32, (64, 128), 0) + (base - 128 + i * 64)

        def one(k, state):
            start, latest, after = state
            end = start + seg_ref[k]
            inside = pos >= start
            return end, jnp.where(inside, start, latest), jnp.where(inside, end, after)

        zero = jnp.zeros((64, 128), jnp.int32)
        _, latest, after = lax.fori_loop(0, NSEG, one, (jnp.int32(0), zero, zero))
        age_ref[at, :] = jnp.where(pos < TOKENS, pos - latest, -1)
        room_ref[at, :] = after - pos
        return carry

    lax.fori_loop(0, 8, chunk, 0)


def in_block(count):
    return lax.rem(lax.broadcasted_iota(jnp.int32, (count, 128), 0), BLK)


def load_inputs(source, pj, first, count):
    def lane(l, carry):
        for b in range(3):
            pj[b, l, first : first + count, :] = source[b, :, lanes(l)].astype(F32)
        return carry

    lax.fori_loop(0, LB, lane, 0)


def features(pj, fw_ref, age_ref, room_ref, feats, xs, xv, prod, first, count):
    def step(at, carry):
        l, r0 = at // count, (first + at % count) * 64
        age = age_ref[rows_at(128 + r0, 64), :]
        inside = in_block(64)
        got = []
        for b in range(3):
            total = pj[b, l, rows_at(PAD + r0, 64), :] * fw_ref[b, 0:1, lanes(l)]
            for i in range(1, 3):
                window = pj[b, l, pl.ds(PAD + r0 - i, 64), :]
                total = total + jnp.where(age >= i, window, 0.0) * fw_ref[b, i : i + 1, lanes(l)]
            feats[b, l, rows_at(r0, 64), :] = total
            got.append(total)
        product = (got[1] * got[2]).astype(BF16)
        wide = product.astype(F32)
        xs[l, rows_at(PAD + r0, 64), :] = wide
        live = room_ref[rows_at(128 + r0, 64), :] >= BLK - inside
        xv[pl.ds(pl.multiple_of(128 + r0, 16), 64), lanes(l)] = jnp.where(live, wide, 0.0).astype(BF16)
        if first:
            prod[pl.ds(pl.multiple_of(r0 - 128, 16), 64), lanes(l)] = product
        return carry

    lax.fori_loop(0, LB * count, step, 0)


def mask_halo(phalo_ref, room_ref, xv):
    def step(at, carry):
        l, r0 = at // 2, (at % 2) * 64
        live = room_ref[rows_at(r0, 64), :] >= BLK - in_block(64)
        rows = pl.ds(pl.multiple_of(r0, 16), 64)
        xv[rows, lanes(l)] = jnp.where(live, phalo_ref[rows, lanes(l)].astype(F32), 0.0).astype(BF16)
        return carry

    lax.fori_loop(0, LB * 2, step, 0)


def chunk_cols(c):
    return pl.ds(pl.multiple_of(c * 256, 256), 256)


def transform(table, source, target, group, c):
    target[group * 256 : (group + 1) * 256, chunk_cols(c)] = jnp.dot(
        table, source[group * 128 : (group + 1) * 128, chunk_cols(c)], preferred_element_type=F32
    )


def all_chunks(act):
    def step(c, carry):
        act(c)
        return carry

    lax.fori_loop(0, CHUNKS, step, 0)


GROUP = 16


def pair(ref, at, l, ft):
    base = at * 32 + ft * 8
    return ref[rows_at(base, 8), lanes(l)], ref[rows_at(base + 16, 8), lanes(l)]


def reach_of(age_ref, m):
    return jnp.broadcast_to(age_ref[pl.ds(128 + m * BLK - 1, 1), :], (8, 128))


def where_pair(live, value):
    return jnp.where(live, value[0], 0.0), jnp.where(live, value[1], 0.0)


def times(a, b):
    return a[0] * b[0] - a[1] * b[1], a[0] * b[1] + a[1] * b[0]


def far_forward(spec_x, spec_g, age_ref, spec_y):
    def outer(at, carry):
        l, ft = at // 2, at % 2
        g = [pair(spec_g, k, l, ft) for k in range(FAR)]

        def inner(q, carry):
            m0 = q * GROUP
            x = [pair(spec_x, m0 + i, l, ft) for i in range(FAR + GROUP - 1)]
            for m in range(GROUP):
                reach = reach_of(age_ref, m0 + m)
                terms = []
                for k in range(1, FAR + 1):
                    terms.append(times(g[k - 1], where_pair(reach >= BLK * (k - 1), x[FAR + m - k])))
                re = sum(t[0] for t in terms[1:]) + terms[0][0]
                im = sum(t[1] for t in terms[1:]) + terms[0][1]
                spec_y[rows_at((m0 + m) * 32 + ft * 8, 8), lanes(l)] = re
                spec_y[rows_at((m0 + m) * 32 + 16 + ft * 8, 8), lanes(l)] = -im
            return carry

        lax.fori_loop(0, ROWS // BLK // GROUP, inner, 0)
        return carry

    lax.fori_loop(0, LB * 2, outer, 0)


def far_back(spec_z, spec_g, age_ref, spec_p, c):
    def outer(at, carry):
        l, ft = c * SPAN + at // 2, at % 2
        g = [pair(spec_g, k, l, ft) for k in range(FAR)]

        def inner(q, carry):
            n0 = q * GROUP
            z = [pair(spec_z, n0 + 1 + i, l, ft) for i in range(FAR + GROUP - 1)]
            reach = [reach_of(age_ref, n0 + 1 + i) for i in range(FAR + GROUP - 1)]
            for n in range(GROUP):
                terms = []
                for k in range(1, FAR + 1):
                    terms.append(times(g[k - 1], where_pair(reach[n + k - 1] >= BLK * (k - 1), z[n + k - 1])))
                re = sum(t[0] for t in terms[1:]) + terms[0][0]
                im = sum(t[1] for t in terms[1:]) + terms[0][1]
                spec_p[rows_at((n0 + n) * 32 + ft * 8, 8), lanes(l)] = re
                spec_p[rows_at((n0 + n) * 32 + 16 + ft * 8, 8), lanes(l)] = -im
            return carry

        lax.fori_loop(0, ROWS // BLK // GROUP, inner, 0)
        return carry

    lax.fori_loop(0, SPAN * 2, outer, 0)


def far_taps(spec_x, spec_z, age_ref, spec_q, c):
    def outer(at, carry):
        l, ft = c * SPAN + at // 2, at % 2

        def inner(q, state):
            m0 = q * GROUP
            x = [pair(spec_x, m0 + i, l, ft) for i in range(FAR + GROUP - 1)]
            for m in range(GROUP):
                reach = reach_of(age_ref, m0 + m)
                z = pair(spec_z, m0 + m, l, ft)
                out = []
                for k in range(1, FAR + 1):
                    re, im = times(where_pair(reach >= BLK * (k - 1), x[FAR + m - k]), z)
                    out += [state[2 * k - 2] + re, state[2 * k - 1] + im]
                state = tuple(out)
            return state

        zero = jnp.zeros((8, 128), F32)
        state = lax.fori_loop(0, ROWS // BLK // GROUP, inner, (zero,) * (2 * FAR))
        for k in range(FAR):
            spec_q[rows_at(k * 32 + ft * 8, 8), lanes(l)] = state[2 * k]
            spec_q[rows_at(k * 32 + 16 + ft * 8, 8), lanes(l)] = -state[2 * k + 1]
        return carry

    lax.fori_loop(0, SPAN * 2, outer, 0)


def inverse(table, source, target, groups, c):
    for group in range(groups):
        target[group * 128 : (group + 1) * 128, chunk_cols(c)] = jnp.dot(
            table, source[group * 256 : (group + 1) * 256, chunk_cols(c)].astype(BF16), preferred_element_type=F32
        )


def near_forward(xs, lf_ref, age_ref, wide, feats, filt, gated):
    def step(at, carry):
        l, r0 = at // 4, (at % 4) * 64
        age = age_ref[rows_at(128 + r0, 64), :]
        inside = in_block(64)
        near = jnp.minimum(age, inside)
        total = jnp.where(age > inside, wide[rows_at(r0, 64), lanes(l)], 0.0)
        for j in range(BLK):
            window = xs[l, pl.ds(PAD + r0 - j, 64), :]
            total = total + jnp.where(near >= j, window, 0.0) * lf_ref[j : j + 1, lanes(l)]
        filt[l, rows_at(r0, 64), :] = total
        gate = feats[0, l, rows_at(r0, 64), :] * total
        gated[pl.ds(pl.multiple_of(r0, 16), 64), lanes(l)] = gate.astype(BF16)
        return carry

    lax.fori_loop(0, LB * 4, step, 0)


def make_long(gg_ref, feats, age_ref, gs_, gl, gv, c):
    def step(at, carry):
        lane, r0 = at // 4, (at % 4) * 64
        l = c * SPAN + lane
        rows = pl.ds(pl.multiple_of(r0, 16), 64)
        sent = (gg_ref[rows, lanes(l)].astype(F32) * feats[0, l, rows_at(r0, 64), :]).astype(BF16)
        long = sent.astype(F32)
        gl[rows, lanes(lane)] = sent
        gs_[l, rows_at(r0, 64), :] = long
        live = age_ref[rows_at(128 + r0, 64), :] > in_block(64)
        gv[rows, lanes(l)] = jnp.where(live, long, 0.0).astype(BF16)
        return carry

    lax.fori_loop(0, SPAN * 4, step, 0)


def mask_next(glhalo_ref, age_ref, gv, c):
    def step(at, carry):
        lane, r0 = at // 2, (at % 2) * 64
        live = age_ref[rows_at(128 + ROWS + r0, 64), :] > in_block(64)
        long = glhalo_ref[pl.ds(pl.multiple_of(r0, 16), 64), lanes(lane)].astype(F32)
        rows = pl.ds(pl.multiple_of(ROWS + r0, 16), 64)
        gv[rows, lanes(c * SPAN + lane)] = jnp.where(live, long, 0.0).astype(BF16)
        return carry

    lax.fori_loop(0, SPAN * 2, step, 0)


def near_back(gs_, xs, lf_ref, age_ref, room_ref, wide, gg_ref, filt, feats, gf, near_taps, c):
    def lane(at, carry):
        l = c * SPAN + at

        def step(i, sums):
            r0 = i * 64
            age = age_ref[rows_at(128 + r0, 64), :]
            room = room_ref[rows_at(128 + r0, 64), :]
            inside = in_block(64)
            near = jnp.minimum(age, inside)
            ahead = jnp.minimum(room, BLK - inside)
            here = gs_[l, rows_at(r0, 64), :]
            total = jnp.where(room >= BLK - inside, wide[rows_at(r0, 64), lanes(l)], 0.0)
            out = []
            for j in range(BLK):
                later = gs_[l, pl.ds(r0 + j, 64), :]
                total = total + jnp.where(ahead > j, later, 0.0) * lf_ref[j : j + 1, lanes(l)]
                window = xs[l, pl.ds(PAD + r0 - j, 64), :]
                both = jnp.where(near >= j, window, 0.0) * here
                out.append(sums[j] + jnp.sum(both.reshape(8, 8, 128), axis=0))
            grad = gg_ref[pl.ds(pl.multiple_of(r0, 16), 64), lanes(l)].astype(F32)
            gf[0, l, rows_at(r0, 64), :] = grad * filt[l, rows_at(r0, 64), :]
            gf[1, l, rows_at(r0, 64), :] = total * feats[2, l, rows_at(r0, 64), :]
            gf[2, l, rows_at(r0, 64), :] = total * feats[1, l, rows_at(r0, 64), :]
            return tuple(out)

        sums = lax.fori_loop(0, 4, step, (jnp.zeros((8, 128), F32),) * BLK)
        for j in range(BLK):
            near_taps[j : j + 1, lanes(l)] = jnp.sum(sums[j], axis=0, keepdims=True)
        return carry

    lax.fori_loop(0, SPAN, lane, 0)


def short_sums(gf, pj, age_ref, short):
    def lane(l, carry):
        def step(i, sums):
            r0 = i * 64
            age = age_ref[rows_at(128 + r0, 64), :]
            out = []
            for b in range(3):
                here = gf[b, l, rows_at(r0, 64), :]
                for tap in range(3):
                    window = pj[b, l, pl.ds(PAD + r0 - tap, 64), :]
                    if tap:
                        window = jnp.where(age >= tap, window, 0.0)
                    out.append(sums[b * 3 + tap] + jnp.sum((here * window).reshape(8, 8, 128), axis=0))
            return tuple(out)

        sums = lax.fori_loop(0, 4, step, (jnp.zeros((8, 128), F32),) * 9)
        for at in range(9):
            short[at : at + 1, lanes(l)] = jnp.sum(sums[at], axis=0, keepdims=True)
        return carry

    lax.fori_loop(0, LB, lane, 0)


def input_grads(gf, fw_ref, room_ref, gproj_ref):
    def step(at, carry):
        l, r0 = at // 4, (at % 4) * 64
        room = room_ref[rows_at(128 + r0, 64), :]
        for b in range(3):
            total = gf[b, l, rows_at(r0, 64), :] * fw_ref[b, 0:1, lanes(l)]
            for tap in range(1, 3):
                later = gf[b, l, pl.ds(r0 + tap, 64), :]
                total = total + jnp.where(room > tap, later, 0.0) * fw_ref[b, tap : tap + 1, lanes(l)]
            gproj_ref[b, pl.ds(pl.multiple_of(r0, 16), 64), lanes(l)] = total.astype(BF16)
        return carry

    lax.fori_loop(0, LB * 4, step, 0)


MESH = pl.DeviceIdType.MESH
NX = 4
COLS = 384
WIDE = NX * COLS
OWN = 32
PEERS = 16


def turned(at, by):
    return lax.rem(at + by + 2 * NX, NX)


class Bag:
    pass


LANED = (LB, ROWS, 128)
PADDED = (LB, PAD + ROWS, 128)
SPEC = (3 * 256, CH)
AGE = (512, 128)
PART = (ROWS, CH // CHUNKS)
BLOCK = (OWN, WIDE)
ROLES = ("own", "back", "fore", "far")
PLACES = dict(
    pj=((3,) + PADDED, F32), feats=((3,) + LANED, F32), filt=(LANED, F32), xs=(PADDED, F32),
    xv=((128 + ROWS, CH), BF16), prod=((128, CH), BF16), jhalo=((3, 16, CH), BF16), phalo=((128, CH), BF16),
    age=(AGE, jnp.int32), room=(AGE, jnp.int32), lfb=((128, CH), BF16), spec_x=(SPEC, F32),
    spec_g=((256, CH), F32), spec_y=((512, CH), F32), wide=((ROWS, CH), F32), gs=(PADDED, F32),
    gv=((ROWS + 128, CH), BF16), spec_z=(SPEC, F32), spec_q=((256, CH), F32), gf=((3,) + PADDED, F32),
    gfhalo=((3, LB, 8, 128), F32), taps=((128, CH), F32), near_taps=((BLK, CH), F32), short=((16, CH), F32),
    cg=((8, 4) + BLOCK, BF16), gg=((ROWS, CH), BF16),
    pk=((PEERS, 16, 640), BF16), rk=((PEERS, 16, 640), BF16), tot=((16, 640), BF16), fk=((PEERS, 16, 640), BF16),
)
for _c in range(CHUNKS):
    PLACES["wg%d" % _c] = ((NX, CH // CHUNKS, COLS), BF16)
    PLACES["gl%d" % _c] = (PART, BF16)
    PLACES["glhalo%d" % _c] = ((128, CH // CHUNKS), BF16)
    for _r in ROLES:
        PLACES["part_%s%d" % (_r, _c)] = (PART, BF16)
    for _r in "abct":
        PLACES["rs_%s%d" % (_r, _c)] = (PART, BF16)
for _r in ROLES:
    PLACES["ga_" + _r] = ((ROWS, CH), BF16)
    PLACES["ob_" + _r] = ((4, 2) + BLOCK, BF16)
    PLACES["co_" + _r] = ((4,) + BLOCK, BF16)
    PLACES["sb_" + _r] = ((4,) + BLOCK, BF16)
    for _k in "abct":
        PLACES["y%s_%s" % (_k, _r)] = (BLOCK, BF16)
    PLACES["rb_" + _r] = (BLOCK, BF16)
    PLACES["fin_" + _r] = (BLOCK, BF16)
SLOTS = 96


def kernel(
    seg_ref, proj_ref, fw_ref, lf_ref, w_ref, cot_ref, tab_ref, tabt_ref,
    out_ref, gproj_ref, taps_ref, short_ref, *scratch,
):
    s = Bag()
    for name, ref in zip(PLACES, scratch):
        setattr(s, name, ref)
    send, recv, t_send, t_recv, u_send, u_recv = scratch[len(PLACES) :]

    def of(name, which):
        return getattr(s, name + str(which))

    ctx, tp = lax.axis_index("ctx"), lax.axis_index("tp")
    z, x, y, core = ctx // 4, ctx % 4, tp // 2, tp % 2
    way = 1 - 2 * core
    other = (ctx, y * 2 + (1 - core))

    def at_x(by):
        return (z * 4 + turned(x, by), tp)

    def at_z(by):
        return (turned(z, by) * 4 + x, tp)

    def at_y(by):
        return (ctx, turned(y, by) * 2 + core)

    def at_ctx(by):
        return (lax.rem(ctx + by + PEERS, PEERS), tp)

    barrier = pltpu.get_barrier_semaphore()
    for by in range(1, PEERS):
        pl.semaphore_signal(barrier, inc=1, device_id=at_ctx(by), device_id_type=MESH)
    for peer in (at_y(1), at_y(-1), other):
        pl.semaphore_signal(barrier, inc=1, device_id=peer, device_id_type=MESH)
    pl.semaphore_wait(barrier, PEERS + 2)

    started = []

    def remote(source, target, peer):
        slot = len(started)
        copy = pltpu.make_async_remote_copy(
            src_ref=source, dst_ref=target, send_sem=send.at[slot], recv_sem=recv.at[slot],
            device_id=peer, device_id_type=MESH,
        )
        copy.start()
        started.append(copy)
        return copy

    def z_cols(by):
        return pl.ds(pl.multiple_of(turned(z, by) * WIDE, 128), WIDE)

    def slab(by):
        return cg.at[turned(y, by) * 2 + core]

    def rest(by):
        return cg.at[turned(y, by) * 2 + core, pl.ds(1, 3)]

    cg = s.cg
    mine = cot_ref.at[:, z_cols(0)]
    c_ahead = remote(mine, cg.at[tp, 0], at_y(way))
    c_behind = remote(mine, cg.at[tp, 0], at_y(-way))
    cot_in = [remote(cot_ref.at[:, z_cols(by)], cg.at[tp, 4 - by], at_z(by)) for by in (1, 3, 2)]
    j_copy = remote(proj_ref.at[:, pl.ds(ROWS - 16, 16), :], s.jhalo, at_ctx(1))
    w_ahead, w_behind, w_on = [], [], []
    for c in range(CHUNKS):
        rows = w_ref.at[pl.ds(c * 256, 256), :]
        w_ahead.append(remote(rows, of("wg", c).at[x], at_x(way)))
        w_behind.append(remote(rows, of("wg", c).at[x], at_x(-way)))
    core_copies = [remote(mine, cg.at[tp, 0], other)]
    for c in range(CHUNKS):
        of("wg", c)[x] = w_ref[c * 256 : (c + 1) * 256, :]
    cg[tp, 0] = cot_ref[:, z_cols(0)]

    find_ages(seg_ref, ctx * ROWS, s.age, s.room)
    load_inputs(proj_ref, s.pj, PAD, ROWS)
    s.xs[:, 0:PAD, :] = jnp.zeros((LB, PAD, 128), F32)
    features(s.pj, fw_ref, s.age, s.room, s.feats, s.xs, s.xv, s.prod, 2, 2)
    p_copy = remote(s.prod, s.phalo, at_ctx(1))

    s.lfb[...] = lf_ref[...].astype(BF16)
    all_chunks(lambda c: transform(tab_ref[2], s.lfb, s.spec_g, 0, c))
    c_ahead.wait_recv()
    c_on = remote(cg.at[turned(y, -way) * 2 + core, 0], cg.at[turned(y, -way) * 2 + core, 0], at_y(way))
    for copy in cot_in:
        copy.wait_recv()
    d_ahead = remote(rest(0), rest(0), at_y(way))
    d_behind = remote(rest(0), rest(0), at_y(-way))
    core_copies.append(remote(rest(0), rest(0), other))

    j_copy.wait_recv()
    load_inputs(s.jhalo, s.pj, 0, PAD)
    features(s.pj, fw_ref, s.age, s.room, s.feats, s.xs, s.xv, s.prod, 0, 2)
    for group in (1, 2):
        all_chunks(lambda c, group=group: transform(tab_ref[0], s.xv, s.spec_x, group, c))

    p_copy.wait_recv()
    mask_halo(s.phalo, s.room, s.xv)
    all_chunks(lambda c: transform(tab_ref[0], s.xv, s.spec_x, 0, c))
    far_forward(s.spec_x, s.spec_g, s.age, s.spec_y)
    d_ahead.wait_recv()
    d_on = remote(rest(-way), rest(-way), at_y(way))
    core_copies.append(remote(slab(-way), slab(-way), other))
    all_chunks(lambda c: inverse(tabt_ref[1], s.spec_y, s.wide, 2, c))
    near_forward(s.xs, lf_ref, s.age, s.wide, s.feats, s.filt, s.ga_own)
    ga_ahead = remote(s.ga_own, s.ga_back, at_z(way))
    ga_behind = remote(s.ga_own, s.ga_fore, at_z(-way))

    for c in range(CHUNKS):
        w_ahead[c].wait_recv()
        passed = of("wg", c).at[turned(x, -way)]
        w_on.append(remote(passed, passed, at_x(way)))
    c_behind.wait_recv()
    d_behind.wait_recv()
    core_copies.append(remote(slab(way), slab(way), other))
    c_on.wait_recv()
    d_on.wait_recv()
    core_copies.append(remote(slab(2), slab(2), other))
    for copy in core_copies:
        copy.wait_recv()

    def backward_part(c, by, target):
        block = turned(0, by)
        total = jnp.zeros(PART, F32)
        for at in range(NX):
            total = total + lax.dot_general(
                cg[:, block, :, at * COLS : (at + 1) * COLS].reshape(ROWS, COLS), of("wg", c)[at],
                (((1,), (1,)), ((), ())), preferred_element_type=F32,
            )
        target[...] = total.astype(BF16)

    def add_rows(target, terms):
        def step(i, carry):
            rows = pl.ds(pl.multiple_of(i * 64, 64), 64)
            total = terms[0][rows, :].astype(F32)
            for term in terms[1:]:
                total = total + term[rows, :].astype(F32)
            target(rows, total.astype(BF16))
            return carry

        lax.fori_loop(0, ROWS // 64, step, 0)

    s_a, s_b, s_c = [], [], []
    for c in range(CHUNKS):
        w_behind[c].wait_recv()
        w_on[c].wait_recv()
        backward_part(c, 2, of("part_far", c))
        s_a.append(remote(of("part_far", c), of("rs_a", c), at_z(way)))
        backward_part(c, -way, of("part_back", c))
        s_b.append(remote(of("part_back", c), of("rs_b", c), at_z(-way)))
        backward_part(c, way, of("part_fore", c))
        backward_part(c, 0, of("part_own", c))

    def forward_part(rows, target):
        def step(at, carry):
            got = jnp.zeros((ROWS, COLS), F32)
            for c in range(CHUNKS):
                got = got + jnp.dot(
                    rows[:, c * 256 : (c + 1) * 256], of("wg", c)[at], preferred_element_type=F32
                )
            cols = pl.ds(pl.multiple_of(at * COLS, 128), COLS)
            target[:, :, :, cols] = got.astype(BF16).reshape(4, 2, OWN, COLS)
            return carry

        lax.fori_loop(0, NX, step, 0)

    there = dict(own="own", back="fore", fore="back", far="far")
    o_core, y_copies, outs = {}, {}, []

    def forward_role(role):
        forward_part(of("ga_", role), of("ob_", role))
        o_core[role] = remote(of("ob_", role).at[:, 1 - core], of("co_", there[role]), other)

    def y_first(role):
        o_core[there[role]].wait_recv()
        ob, co, sb = of("ob_", role), of("co_", role), of("sb_", role)

        def step(q, carry):
            sb[q] = (ob[q, core].astype(F32) + co[q].astype(F32)).astype(BF16)
            return carry

        lax.fori_loop(0, 4, step, 0)
        y_copies[role] = [
            remote(sb.at[turned(y, 2)], of("ya_", role), at_y(way)),
            remote(sb.at[turned(y, -way)], of("yb_", role), at_y(-way)),
        ]

    def y_second(role):
        y_copies[role][0].wait_recv()
        held = of("yt_", role)
        held[...] = (of("ya_", role)[...].astype(F32) + of("sb_", role)[turned(y, way)].astype(F32)).astype(BF16)
        y_copies[role].append(remote(held, of("yc_", role), at_y(way)))

    def y_last(role):
        y_copies[role][1].wait_recv()
        y_copies[role][2].wait_recv()
        total = of("sb_", role)[y].astype(F32) + of("yb_", role)[...].astype(F32) + of("yc_", role)[...].astype(F32)
        of("rb_", role)[...] = total.astype(BF16)
        if role != "own":
            by = dict(back=-way, fore=way, far=2)[role]
            outs.append(remote(of("rb_", role), of("fin_", there[role]), at_z(by)))

    forward_role("own")
    for c in range(CHUNKS):
        s_a[c].wait_recv()
        held = of("rs_t", c)

        def put(rows, value, held=held):
            held[rows, :] = value

        add_rows(put, (of("rs_a", c), of("part_fore", c)))
        s_c.append(remote(held, of("rs_c", c), at_z(way)))
    ga_ahead.wait_recv()
    ga_on = remote(s.ga_back, s.ga_far, at_z(way))
    forward_role("back")
    ga_behind.wait_recv()
    forward_role("fore")
    y_first("own")

    l_copies = []
    s.gs[:, ROWS : ROWS + PAD, :] = jnp.zeros((LB, PAD, 128), F32)

    def back_first(c):
        s_b[c].wait_recv()
        s_c[c].wait_recv()

        def put(rows, value):
            s.gg[rows, c * 256 : (c + 1) * 256] = value

        add_rows(put, (of("part_own", c), of("rs_b", c), of("rs_c", c)))
        make_long(s.gg, s.feats, s.age, s.gs, of("gl", c), s.gv, c)
        l_copies.append(remote(of("gl", c).at[pl.ds(0, 128), :], of("glhalo", c), at_ctx(-1)))
        for group in (0, 1):
            transform(tab_ref[1], s.gv, s.spec_z, group, c)
        far_taps(s.spec_x, s.spec_z, s.age, s.spec_q, c)

    def back_second(c):
        l_copies[c].wait_recv()
        mask_next(of("glhalo", c), s.age, s.gv, c)
        transform(tab_ref[1], s.gv, s.spec_z, 2, c)
        far_back(s.spec_z, s.spec_g, s.age, s.spec_y, c)
        inverse(tabt_ref[0], s.spec_y, s.wide, 2, c)
        near_back(
            s.gs, s.xs, lf_ref, s.age, s.room, s.wide, s.gg, s.filt, s.feats, s.gf, s.near_taps, c
        )
        inverse(tabt_ref[2], s.spec_q, s.taps, 1, c)
        cols = pl.ds(c * 256, 256)
        s.taps[0:BLK, cols] = s.taps[0:BLK, cols] + s.near_taps[:, cols]

    back_first(0)
    y_first("back")
    y_first("fore")
    y_second("own")
    back_first(1)
    back_second(0)
    ga_on.wait_recv()
    forward_role("far")
    y_second("back")
    y_second("fore")
    back_first(2)
    y_first("far")
    y_last("own")
    back_second(1)
    y_last("back")
    y_last("fore")
    back_first(3)
    y_second("far")
    back_second(2)
    back_second(3)
    f_copy = remote(s.gf.at[:, :, pl.ds(0, 8), :], s.gfhalo, at_ctx(-1))
    y_last("far")

    short_sums(s.gf, s.pj, s.age, s.short)
    for q in range(PEERS):
        rows = s.taps[q * 8 : (q + 1) * 8, :]
        s.pk[q, :, 0:512] = jnp.concatenate([rows[:, 0:512], rows[:, 512:1024]], axis=0).astype(BF16)
        if q < 9:
            row = [s.short[q : q + 1, i * 128 : (i + 1) * 128] for i in range(8)]
            row.append(jnp.zeros((8, 128), F32))
            s.pk[q, :, 512:640] = jnp.concatenate(row, axis=0).astype(BF16)
        else:
            s.pk[q, :, 512:640] = jnp.zeros((16, 128), BF16)

    def tap_copy(i):
        peer = lax.rem(ctx + i, PEERS)
        return pltpu.make_async_remote_copy(
            src_ref=s.pk.at[peer], dst_ref=s.rk.at[i], send_sem=t_send.at[i], recv_sem=t_recv.at[i],
            device_id=(peer, tp), device_id_type=MESH,
        )

    def total_copy(i):
        peer = lax.rem(ctx + i, PEERS)
        return pltpu.make_async_remote_copy(
            src_ref=s.tot, dst_ref=s.fk.at[ctx], send_sem=u_send.at[i], recv_sem=u_recv.at[i],
            device_id=(peer, tp), device_id_type=MESH,
        )

    def each(make, act):
        def step(i, carry):
            act(make(i))
            return carry

        lax.fori_loop(1, PEERS, step, 0)

    each(tap_copy, lambda copy: copy.start())
    f_copy.wait_recv()
    s.gf[:, :, ROWS : ROWS + 8, :] = s.gfhalo[...]
    input_grads(s.gf, fw_ref, s.room, gproj_ref)
    each(tap_copy, lambda copy: copy.wait_recv())
    total = s.pk[ctx].astype(F32)
    for i in range(1, PEERS):
        total = total + s.rk[i].astype(F32)
    s.tot[...] = total.astype(BF16)
    s.fk[ctx] = s.tot[...]
    each(total_copy, lambda copy: copy.start())

    for copy in outs:
        copy.wait_recv()
    out_ref[:, z_cols(0)] = s.rb_own[...]
    for by, role in ((-way, "back"), (way, "fore"), (2, "far")):
        out_ref[:, z_cols(by)] = of("fin_", role)[...]

    each(total_copy, lambda copy: copy.wait_recv())
    norm = TOKENS**-0.5
    for q in range(PEERS):
        done = s.fk[q].astype(F32) * norm
        taps_ref[q * 8 : (q + 1) * 8, 0:512] = done[0:8, 0:512]
        taps_ref[q * 8 : (q + 1) * 8, 512:1024] = done[8:16, 0:512]
        if q < 9:
            for i in range(8):
                short_ref[q // 3, q % 3 : q % 3 + 1, i * 128 : (i + 1) * 128] = done[i : i + 1, 512:640]

    each(tap_copy, lambda copy: copy.wait_send())
    each(total_copy, lambda copy: copy.wait_send())
    for copy in started:
        copy.wait_send()


def hand_over(*refs):
    count = len(refs) // 2
    for i in range(count):
        refs[count + i][...] = refs[i][...]


def shards(projected, feat_weight, long_filter, out_weight, seg_lengths, cotangent):
    tab, tabt = (jnp.asarray(t) for t in tables())
    vm = pl.BlockSpec(memory_space=pltpu.VMEM)
    dma = pltpu.SemaphoreType.DMA
    outs = [
        jax.ShapeDtypeStruct((OWN, 4 * WIDE), BF16),
        jax.ShapeDtypeStruct((3, ROWS, CH), BF16),
        jax.ShapeDtypeStruct((128, CH), F32),
        jax.ShapeDtypeStruct((3, 3, CH), F32),
    ]
    results = pl.pallas_call(
        kernel,
        out_shape=outs,
        in_specs=[pl.BlockSpec(memory_space=pltpu.SMEM)] + [vm] * 7,
        out_specs=[vm] * 4,
        scratch_shapes=[pltpu.VMEM(shape, kind) for shape, kind in PLACES.values()]
        + [dma((SLOTS,)), dma((SLOTS,)), dma((PEERS,)), dma((PEERS,)), dma((PEERS,)), dma((PEERS,))],
        compiler_params=pltpu.CompilerParams(
            collective_id=0, has_side_effects=True, vmem_limit_bytes=60 * 2**20
        ),
    )(seg_lengths, projected, feat_weight, long_filter, out_weight, cotangent, tab, tabt)
    return tuple(
        pl.pallas_call(hand_over, out_shape=outs, in_specs=[vm] * 4, out_specs=[vm] * 4)(*results)
    )


def solution(mesh):
    return jax.shard_map(
        shards,
        mesh=mesh,
        in_specs=(
            P(None, "ctx", "tp"),
            P(None, None, "tp"),
            P(None, "tp"),
            P("tp", "ctx"),
            P(),
            P(("ctx", "tp"), None),
        ),
        out_specs=(
            P(("ctx", "tp"), None),
            P(None, "ctx", "tp"),
            P(None, "tp"),
            P(None, None, "tp"),
        ),
        check_vma=False,
    )
```

time: 144 us -> 118 us (0.82)
  Pallas kernels: 137 us -> 117 us
  local copies, waits for them, and re-layouts: 5.91 us -> 0 us
    pallas_call x1 -> x2, Pallas kernels: 137 us -> 117 us  [the longest x1 114 us: shards(): pl.pallas_call(kernel, out_shape=outs, in_specs=[pl.BlockSpec(memory_spac...]
    unnamed x8 -> x0, local copies, waits for them, and re-layouts: 5.91 us -> none
where the time goes in v3:
time: 118 us
  Pallas kernels  117 us (99%)
    pallas_call x1, Pallas kernels, shards(): pl.pallas_call(kernel, out_shape=outs, in_specs=[pl.BlockSpec(memory_spac...  114 us
    pallas_call x1, Pallas kernels, shards(): pl.pallas_call(hand_over, out_shape=outs, in_specs=[vm] * 4, out_specs=[v...  3.18 us

profile of v3, /device:TPU:0, one launch (start us, length us, event | category | flops | bytes accessed | tf_op | source)
XLA Modules:
  0.0 117.5 jit_solution(3005706591298960393)
XLA Ops:
  0.6 113.7 %shard_map.111 = (bf16[32,6144]{1,0:T(8,128)(2,1)}, bf16[3,256,1024]{2,1,0:T(8,128)(2,1)}, f32[128,1024]{1,0:T(8,128)}, f32[3,3,1024]{2,1,0:T(4,128)}) custom-call(s32[32]{0:T(128)} %seg_ref.1, bf16[3,256,1024]{2,1,0:T(8,128)(2,1)} %proj_ref.1, f32[3,3,1024]{2,1,0:T(4,128)} %fw_ref.1, f32[128,1024]{1,0:T(8,128)} %lf_ref.1, bf16[1024,384]{1,0:T(8,128)(2,1)} %w_ref.1, ...), custom_call_target="tpu_custom_call" | custom-call | tf_op jit(solution)/shard_map/pallas_call | solution.py:766
  114.4 3.2 %shard_map.112 = (bf16[32,6144]{1,0:T(8,128)(2,1)}, bf16[3,256,1024]{2,1,0:T(8,128)(2,1)}, f32[128,1024]{1,0:T(8,128)}, f32[3,3,1024]{2,1,0:T(4,128)}) custom-call(bf16[32,6144]{1,0:T(8,128)(2,1)} %get-tuple-element.8.refs_0_, bf16[3,256,1024]{2,1,0:T(8,128)(2,1)} %get-tuple-element.9.refs_1_, f32[128,1024]{1,0:T(8,128)} %get-tuple-element.10.refs_2_, ...), custom_call_target="tpu_custom_call" | custom-call | tf_op jit(solution)/shard_map/pallas_call | solution.py:778

commit v4 on v3

--- a/solution.py
+++ b/solution.py
@@ -277,7 +277,8 @@
     def step(at, carry):
         lane, r0 = at // 2, (at % 2) * 64
         live = age_ref[rows_at(128 + ROWS + r0, 64), :] > in_block(64)
-        long = glhalo_ref[pl.ds(pl.multiple_of(r0, 16), 64), lanes(lane)].astype(F32)
+        source = pl.ds(pl.multiple_of(r0, 16), 64)
+        long = glhalo_ref[source, lanes(lane)].astype(F32)
         rows = pl.ds(pl.multiple_of(ROWS + r0, 16), 64)
         gv[rows, lanes(c * SPAN + lane)] = jnp.where(live, long, 0.0).astype(BF16)
         return carry
@@ -319,8 +320,10 @@
     lax.fori_loop(0, SPAN, lane, 0)
 
 
-def short_sums(gf, pj, age_ref, short):
-    def lane(l, carry):
+def short_sums(gf, pj, age_ref, short, c):
+    def lane(at_lane, carry):
+        l = c * SPAN + at_lane
+
         def step(i, sums):
             r0 = i * 64
             age = age_ref[rows_at(128 + r0, 64), :]
@@ -339,12 +342,12 @@
             short[at : at + 1, lanes(l)] = jnp.sum(sums[at], axis=0, keepdims=True)
         return carry
 
-    lax.fori_loop(0, LB, lane, 0)
-
-
-def input_grads(gf, fw_ref, room_ref, gproj_ref):
+    lax.fori_loop(0, SPAN, lane, 0)
+
+
+def input_grads(gf, fw_ref, room_ref, gproj_ref, c):
     def step(at, carry):
-        l, r0 = at // 4, (at % 4) * 64
+        l, r0 = c * SPAN + at // 4, (at % 4) * 64
         room = room_ref[rows_at(128 + r0, 64), :]
         for b in range(3):
             total = gf[b, l, rows_at(r0, 64), :] * fw_ref[b, 0:1, lanes(l)]
@@ -354,7 +357,7 @@
             gproj_ref[b, pl.ds(pl.multiple_of(r0, 16), 64), lanes(l)] = total.astype(BF16)
         return carry
 
-    lax.fori_loop(0, LB * 4, step, 0)
+    lax.fori_loop(0, SPAN * 4, step, 0)
 
 
 MESH = pl.DeviceIdType.MESH
@@ -386,14 +389,18 @@
     age=(AGE, jnp.int32), room=(AGE, jnp.int32), lfb=((128, CH), BF16), spec_x=(SPEC, F32),
     spec_g=((256, CH), F32), spec_y=((512, CH), F32), wide=((ROWS, CH), F32), gs=(PADDED, F32),
     gv=((ROWS + 128, CH), BF16), spec_z=(SPEC, F32), spec_q=((256, CH), F32), gf=((3,) + PADDED, F32),
-    gfhalo=((3, LB, 8, 128), F32), taps=((128, CH), F32), near_taps=((BLK, CH), F32), short=((16, CH), F32),
+    taps=((128, CH), F32), near_taps=((BLK, CH), F32), short=((16, CH), F32),
     cg=((8, 4) + BLOCK, BF16), gg=((ROWS, CH), BF16),
-    pk=((PEERS, 16, 640), BF16), rk=((PEERS, 16, 640), BF16), tot=((16, 640), BF16), fk=((PEERS, 16, 640), BF16),
 )
+for _h, _w in ((0, 256), (1, 384)):
+    for _k in ("pk", "rk", "fk"):
+        PLACES["%s%d" % (_k, _h)] = ((PEERS, 16, _w), BF16)
+    PLACES["tot%d" % _h] = ((16, _w), BF16)
 for _c in range(CHUNKS):
     PLACES["wg%d" % _c] = ((NX, CH // CHUNKS, COLS), BF16)
     PLACES["gl%d" % _c] = (PART, BF16)
     PLACES["glhalo%d" % _c] = ((128, CH // CHUNKS), BF16)
+    PLACES["gfhalo%d" % _c] = ((3, SPAN, 8, 128), F32)
     for _r in ROLES:
         PLACES["part_%s%d" % (_r, _c)] = (PART, BF16)
     for _r in "abct":
@@ -474,10 +481,18 @@
     cot_in = [remote(cot_ref.at[:, z_cols(by)], cg.at[tp, 4 - by], at_z(by)) for by in (1, 3, 2)]
     j_copy = remote(proj_ref.at[:, pl.ds(ROWS - 16, 16), :], s.jhalo, at_ctx(1))
     w_ahead, w_behind, w_on = [], [], []
-    for c in range(CHUNKS):
+
+    def w_send(c):
         rows = w_ref.at[pl.ds(c * 256, 256), :]
         w_ahead.append(remote(rows, of("wg", c).at[x], at_x(way)))
         w_behind.append(remote(rows, of("wg", c).at[x], at_x(-way)))
+
+    def w_pass(c):
+        w_ahead[c].wait_recv()
+        passed = of("wg", c).at[turned(x, -way)]
+        w_on.append(remote(passed, passed, at_x(way)))
+
+    w_send(0)
     core_copies = [remote(mine, cg.at[tp, 0], other)]
     for c in range(CHUNKS):
         of("wg", c)[x] = w_ref[c * 256 : (c + 1) * 256, :]
@@ -489,6 +504,9 @@
     features(s.pj, fw_ref, s.age, s.room, s.feats, s.xs, s.xv, s.prod, 2, 2)
     p_copy = remote(s.prod, s.phalo, at_ctx(1))
 
+    w_send(1)
+    w_send(2)
+    w_send(3)
     s.lfb[...] = lf_ref[...].astype(BF16)
     all_chunks(lambda c: transform(tab_ref[2], s.lfb, s.spec_g, 0, c))
     c_ahead.wait_recv()
@@ -518,9 +536,7 @@
     ga_behind = remote(s.ga_own, s.ga_fore, at_z(-way))
 
     for c in range(CHUNKS):
-        w_ahead[c].wait_recv()
-        passed = of("wg", c).at[turned(x, -way)]
-        w_on.append(remote(passed, passed, at_x(way)))
+        w_pass(c)
     c_behind.wait_recv()
     d_behind.wait_recv()
     core_copies.append(remote(slab(way), slab(way), other))
@@ -645,6 +661,8 @@
             transform(tab_ref[1], s.gv, s.spec_z, group, c)
         far_taps(s.spec_x, s.spec_z, s.age, s.spec_q, c)
 
+    f_copies = []
+
     def back_second(c):
         l_copies[c].wait_recv()
         mask_next(of("glhalo", c), s.age, s.gv, c)
@@ -654,95 +672,122 @@
         near_back(
             s.gs, s.xs, lf_ref, s.age, s.room, s.wide, s.gg, s.filt, s.feats, s.gf, s.near_taps, c
         )
+        f_copies.append(
+            remote(s.gf.at[:, pl.ds(c * SPAN, SPAN), pl.ds(0, 8), :], of("gfhalo", c), at_ctx(-1))
+        )
         inverse(tabt_ref[2], s.spec_q, s.taps, 1, c)
         cols = pl.ds(c * 256, 256)
         s.taps[0:BLK, cols] = s.taps[0:BLK, cols] + s.near_taps[:, cols]
+        short_sums(s.gf, s.pj, s.age, s.short, c)
+
+    def back_third(c):
+        f_copies[c].wait_recv()
+        s.gf[:, c * SPAN : (c + 1) * SPAN, ROWS : ROWS + 8, :] = of("gfhalo", c)[...]
+        input_grads(s.gf, fw_ref, s.room, gproj_ref, c)
+
+    def pack(h):
+        pk = of("pk", h)
+        for q in range(PEERS):
+            rows = s.taps[q * 8 : (q + 1) * 8, h * 512 : (h + 1) * 512]
+            pk[q, :, 0:256] = jnp.concatenate([rows[:, 0:256], rows[:, 256:512]], axis=0).astype(BF16)
+            if h and q < 9:
+                row = [s.short[q : q + 1, i * 128 : (i + 1) * 128] for i in range(8)]
+                row.append(jnp.zeros((8, 128), F32))
+                pk[q, :, 256:384] = jnp.concatenate(row, axis=0).astype(BF16)
+            elif h:
+                pk[q, :, 256:384] = jnp.zeros((16, 128), BF16)
+
+    def tap_copy(h):
+        def make(i):
+            peer = lax.rem(ctx + i, PEERS)
+            return pltpu.make_async_remote_copy(
+                src_ref=of("pk", h).at[peer], dst_ref=of("rk", h).at[i], send_sem=t_send.at[h, i],
+                recv_sem=t_recv.at[h, i], device_id=(peer, tp), device_id_type=MESH,
+            )
+
+        return make
+
+    def total_copy(h):
+        def make(i):
+            peer = lax.rem(ctx + i, PEERS)
+            return pltpu.make_async_remote_copy(
+                src_ref=of("tot", h), dst_ref=of("fk", h).at[ctx], send_sem=u_send.at[h, i],
+                recv_sem=u_recv.at[h, i], device_id=(peer, tp), device_id_type=MESH,
+            )
+
+        return make
+
+    def each(make, act):
+        def step(i, carry):
+            act(make(i))
+            return carry
+
+        lax.fori_loop(1, PEERS, step, 0)
+
+    def send_taps(h):
+        pack(h)
+        each(tap_copy(h), lambda copy: copy.start())
+
+    def sum_taps(h):
+        each(tap_copy(h), lambda copy: copy.wait_recv())
+        total = of("pk", h)[ctx].astype(F32)
+        for i in range(1, PEERS):
+            total = total + of("rk", h)[i].astype(F32)
+        of("tot", h)[...] = total.astype(BF16)
+        of("fk", h)[ctx] = of("tot", h)[...]
+        each(total_copy(h), lambda copy: copy.start())
+
+    def finish_taps(h):
+        each(total_copy(h), lambda copy: copy.wait_recv())
+        norm = TOKENS**-0.5
+        for q in range(PEERS):
+            done = of("fk", h)[q].astype(F32) * norm
+            taps_ref[q * 8 : (q + 1) * 8, h * 512 : h * 512 + 256] = done[0:8, 0:256]
+            taps_ref[q * 8 : (q + 1) * 8, h * 512 + 256 : (h + 1) * 512] = done[8:16, 0:256]
+            if h and q < 9:
+                for i in range(8):
+                    short_ref[q // 3, q % 3 : q % 3 + 1, i * 128 : (i + 1) * 128] = done[i : i + 1, 256:384]
 
     back_first(0)
     y_first("back")
     y_first("fore")
     y_second("own")
     back_first(1)
-    back_second(0)
     ga_on.wait_recv()
     forward_role("far")
     y_second("back")
     y_second("fore")
+    back_second(0)
     back_first(2)
     y_first("far")
     y_last("own")
     back_second(1)
+    send_taps(0)
     y_last("back")
     y_last("fore")
     back_first(3)
     y_second("far")
     back_second(2)
+    sum_taps(0)
+    back_third(0)
+    y_last("far")
     back_second(3)
-    f_copy = remote(s.gf.at[:, :, pl.ds(0, 8), :], s.gfhalo, at_ctx(-1))
-    y_last("far")
-
-    short_sums(s.gf, s.pj, s.age, s.short)
-    for q in range(PEERS):
-        rows = s.taps[q * 8 : (q + 1) * 8, :]
-        s.pk[q, :, 0:512] = jnp.concatenate([rows[:, 0:512], rows[:, 512:1024]], axis=0).astype(BF16)
-        if q < 9:
-            row = [s.short[q : q + 1, i * 128 : (i + 1) * 128] for i in range(8)]
-            row.append(jnp.zeros((8, 128), F32))
-            s.pk[q, :, 512:640] = jnp.concatenate(row, axis=0).astype(BF16)
-        else:
-            s.pk[q, :, 512:640] = jnp.zeros((16, 128), BF16)
-
-    def tap_copy(i):
-        peer = lax.rem(ctx + i, PEERS)
-        return pltpu.make_async_remote_copy(
-            src_ref=s.pk.at[peer], dst_ref=s.rk.at[i], send_sem=t_send.at[i], recv_sem=t_recv.at[i],
-            device_id=(peer, tp), device_id_type=MESH,
-        )
-
-    def total_copy(i):
-        peer = lax.rem(ctx + i, PEERS)
-        return pltpu.make_async_remote_copy(
-            src_ref=s.tot, dst_ref=s.fk.at[ctx], send_sem=u_send.at[i], recv_sem=u_recv.at[i],
-            device_id=(peer, tp), device_id_type=MESH,
-        )
-
-    def each(make, act):
-        def step(i, carry):
-            act(make(i))
-            return carry
-
-        lax.fori_loop(1, PEERS, step, 0)
-
-    each(tap_copy, lambda copy: copy.start())
-    f_copy.wait_recv()
-    s.gf[:, :, ROWS : ROWS + 8, :] = s.gfhalo[...]
-    input_grads(s.gf, fw_ref, s.room, gproj_ref)
-    each(tap_copy, lambda copy: copy.wait_recv())
-    total = s.pk[ctx].astype(F32)
-    for i in range(1, PEERS):
-        total = total + s.rk[i].astype(F32)
-    s.tot[...] = total.astype(BF16)
-    s.fk[ctx] = s.tot[...]
-    each(total_copy, lambda copy: copy.start())
-
+    send_taps(1)
+    back_third(1)
+    finish_taps(0)
     for copy in outs:
         copy.wait_recv()
     out_ref[:, z_cols(0)] = s.rb_own[...]
     for by, role in ((-way, "back"), (way, "fore"), (2, "far")):
         out_ref[:, z_cols(by)] = of("fin_", role)[...]
-
-    each(total_copy, lambda copy: copy.wait_recv())
-    norm = TOKENS**-0.5
-    for q in range(PEERS):
-        done = s.fk[q].astype(F32) * norm
-        taps_ref[q * 8 : (q + 1) * 8, 0:512] = done[0:8, 0:512]
-        taps_ref[q * 8 : (q + 1) * 8, 512:1024] = done[8:16, 0:512]
-        if q < 9:
-            for i in range(8):
-                short_ref[q // 3, q % 3 : q % 3 + 1, i * 128 : (i + 1) * 128] = done[i : i + 1, 512:640]
-
-    each(tap_copy, lambda copy: copy.wait_send())
-    each(total_copy, lambda copy: copy.wait_send())
+    sum_taps(1)
+    back_third(2)
+    back_third(3)
+    finish_taps(1)
+
+    for h in range(2):
+        each(tap_copy(h), lambda copy: copy.wait_send())
+        each(total_copy(h), lambda copy: copy.wait_send())
     for copy in started:
         copy.wait_send()
 
@@ -769,7 +814,7 @@
         in_specs=[pl.BlockSpec(memory_space=pltpu.SMEM)] + [vm] * 7,
         out_specs=[vm] * 4,
         scratch_shapes=[pltpu.VMEM(shape, kind) for shape, kind in PLACES.values()]
-        + [dma((SLOTS,)), dma((SLOTS,)), dma((PEERS,)), dma((PEERS,)), dma((PEERS,)), dma((PEERS,))],
+        + [dma((SLOTS,)), dma((SLOTS,)), *[dma((2, PEERS))] * 4],
         compiler_params=pltpu.CompilerParams(
             collective_id=0, has_side_effects=True, vmem_limit_bytes=60 * 2**20
         ),

time: 118 us -> 106 us (0.90)
  Pallas kernels: 117 us -> 105 us
    pallas_call x1, Pallas kernels: 114 us -> 102 us  [shards(): pl.pallas_call(kernel, out_shape=outs, in_specs=[pl.BlockSpec(memory_spac...]
where the time goes in v4:
time: 106 us
  Pallas kernels  105 us (99%)
    pallas_call x1, Pallas kernels, shards(): pl.pallas_call(kernel, out_shape=outs, in_specs=[pl.BlockSpec(memory_spac...  102 us
    pallas_call x1, Pallas kernels, shards(): pl.pallas_call(hand_over, out_shape=outs, in_specs=[vm] * 4, out_specs=[v...  3.18 us

profile of v4, /device:TPU:0, one launch (start us, length us, event | category | flops | bytes accessed | tf_op | source)
XLA Modules:
  0.0 105.8 jit_solution(1070087257029560095)
XLA Ops:
  0.6 102.0 %shard_map.111 = (bf16[32,6144]{1,0:T(8,128)(2,1)}, bf16[3,256,1024]{2,1,0:T(8,128)(2,1)}, f32[128,1024]{1,0:T(8,128)}, f32[3,3,1024]{2,1,0:T(4,128)}) custom-call(s32[32]{0:T(128)} %seg_ref.1, bf16[3,256,1024]{2,1,0:T(8,128)(2,1)} %proj_ref.1, f32[3,3,1024]{2,1,0:T(4,128)} %fw_ref.1, f32[128,1024]{1,0:T(8,128)} %lf_ref.1, bf16[1024,384]{1,0:T(8,128)(2,1)} %w_ref.1, ...), custom_call_target="tpu_custom_call" | custom-call | tf_op jit(solution)/shard_map/pallas_call | solution.py:811
  102.6 3.2 %shard_map.112 = (bf16[32,6144]{1,0:T(8,128)(2,1)}, bf16[3,256,1024]{2,1,0:T(8,128)(2,1)}, f32[128,1024]{1,0:T(8,128)}, f32[3,3,1024]{2,1,0:T(4,128)}) custom-call(bf16[32,6144]{1,0:T(8,128)(2,1)} %get-tuple-element.8.refs_0_, bf16[3,256,1024]{2,1,0:T(8,128)(2,1)} %get-tuple-element.9.refs_1_, f32[128,1024]{1,0:T(8,128)} %get-tuple-element.10.refs_2_, ...), custom_call_target="tpu_custom_call" | custom-call | tf_op jit(solution)/shard_map/pallas_call | solution.py:823

commit v5 on v4

--- a/solution.py
+++ b/solution.py
@@ -48,7 +48,7 @@
     return pl.ds(pl.multiple_of(start, 8), count)
 
 
-def find_ages(seg_ref, base, age_ref, room_ref):
+def find_ages(seg_ref, base, age_ref, room_ref, first, last):
     def chunk(i, carry):
         at = rows_at(i * 64, 64)
         pos = lax.broadcasted_iota(jnp.int32, (64, 128), 0) + (base - 128 + i * 64)
@@ -65,17 +65,17 @@
         room_ref[at, :] = after - pos
         return carry
 
-    lax.fori_loop(0, 8, chunk, 0)
+    lax.fori_loop(first, last, chunk, 0)
 
 
 def in_block(count):
     return lax.rem(lax.broadcasted_iota(jnp.int32, (count, 128), 0), BLK)
 
 
-def load_inputs(source, pj, first, count):
+def load_inputs(source, pj, first, count, start=0):
     def lane(l, carry):
         for b in range(3):
-            pj[b, l, first : first + count, :] = source[b, :, lanes(l)].astype(F32)
+            pj[b, l, first : first + count, :] = source[b, start : start + count, lanes(l)].astype(F32)
         return carry
 
     lax.fori_loop(0, LB, lane, 0)
@@ -494,19 +494,22 @@
 
     w_send(0)
     core_copies = [remote(mine, cg.at[tp, 0], other)]
+
+    find_ages(seg_ref, ctx * ROWS, s.age, s.room, 4, 6)
+    load_inputs(proj_ref, s.pj, PAD + 112, ROWS - 112, 112)
+    features(s.pj, fw_ref, s.age, s.room, s.feats, s.xs, s.xv, s.prod, 2, 2)
+    p_copy = remote(s.prod, s.phalo, at_ctx(1))
+
+    w_send(1)
+    w_send(2)
+    w_send(3)
     for c in range(CHUNKS):
         of("wg", c)[x] = w_ref[c * 256 : (c + 1) * 256, :]
     cg[tp, 0] = cot_ref[:, z_cols(0)]
-
-    find_ages(seg_ref, ctx * ROWS, s.age, s.room)
-    load_inputs(proj_ref, s.pj, PAD, ROWS)
+    find_ages(seg_ref, ctx * ROWS, s.age, s.room, 0, 4)
+    find_ages(seg_ref, ctx * ROWS, s.age, s.room, 6, 8)
+    load_inputs(proj_ref, s.pj, PAD, 112)
     s.xs[:, 0:PAD, :] = jnp.zeros((LB, PAD, 128), F32)
-    features(s.pj, fw_ref, s.age, s.room, s.feats, s.xs, s.xv, s.prod, 2, 2)
-    p_copy = remote(s.prod, s.phalo, at_ctx(1))
-
-    w_send(1)
-    w_send(2)
-    w_send(3)
     s.lfb[...] = lf_ref[...].astype(BF16)
     all_chunks(lambda c: transform(tab_ref[2], s.lfb, s.spec_g, 0, c))
     c_ahead.wait_recv()
@@ -567,6 +570,16 @@
 
         lax.fori_loop(0, ROWS // 64, step, 0)
 
+    def reduce_on(c):
+        s_a[c].wait_recv()
+        held = of("rs_t", c)
+
+        def put(rows, value, held=held):
+            held[rows, :] = value
+
+        add_rows(put, (of("rs_a", c), of("part_fore", c)))
+        s_c.append(remote(held, of("rs_c", c), at_z(way)))
+
     s_a, s_b, s_c = [], [], []
     for c in range(CHUNKS):
         w_behind[c].wait_recv()
@@ -577,6 +590,8 @@
         s_b.append(remote(of("part_back", c), of("rs_b", c), at_z(-way)))
         backward_part(c, way, of("part_fore", c))
         backward_part(c, 0, of("part_own", c))
+        if c >= 2:
+            reduce_on(c - 2)
 
     def forward_part(rows, target):
         def step(at, carry):
@@ -628,15 +643,8 @@
             outs.append(remote(of("rb_", role), of("fin_", there[role]), at_z(by)))
 
     forward_role("own")
-    for c in range(CHUNKS):
-        s_a[c].wait_recv()
-        held = of("rs_t", c)
-
-        def put(rows, value, held=held):
-            held[rows, :] = value
-
-        add_rows(put, (of("rs_a", c), of("part_fore", c)))
-        s_c.append(remote(held, of("rs_c", c), at_z(way)))
+    for c in (2, 3):
+        reduce_on(c)
     ga_ahead.wait_recv()
     ga_on = remote(s.ga_back, s.ga_far, at_z(way))
     forward_role("back")
@@ -793,9 +801,25 @@
 
 
 def hand_over(*refs):
-    count = len(refs) // 2
-    for i in range(count):
-        refs[count + i][...] = refs[i][...]
+    sources, targets, held, sem = refs[0:4], refs[4:8], refs[8:12], refs[12]
+    pieces = [(0, None), (2, None), (3, None)] + [(1, b) for b in range(3)]
+
+    def part(ref, at):
+        return ref if at is None else ref.at[at]
+
+    into = [
+        pltpu.make_async_copy(part(sources[i], at), part(held[i], at), sem.at[0, n]) for n, (i, at) in enumerate(pieces)
+    ]
+    back = [
+        pltpu.make_async_copy(part(held[i], at), part(targets[i], at), sem.at[1, n]) for n, (i, at) in enumerate(pieces)
+    ]
+    for copy in into:
+        copy.start()
+    for n, copy in enumerate(into):
+        copy.wait()
+        back[n].start()
+    for copy in back:
+        copy.wait()
 
 
 def shards(projected, feat_weight, long_filter, out_weight, seg_lengths, cotangent):
@@ -819,8 +843,15 @@
             collective_id=0, has_side_effects=True, vmem_limit_bytes=60 * 2**20
         ),
     )(seg_lengths, projected, feat_weight, long_filter, out_weight, cotangent, tab, tabt)
+    anywhere = pl.BlockSpec(memory_space=pl.ANY)
     return tuple(
-        pl.pallas_call(hand_over, out_shape=outs, in_specs=[vm] * 4, out_specs=[vm] * 4)(*results)
+        pl.pallas_call(
+            hand_over,
+            out_shape=outs,
+            in_specs=[anywhere] * 4,
+            out_specs=[anywhere] * 4,
+            scratch_shapes=[pltpu.VMEM(o.shape, o.dtype) for o in outs] + [dma((2, 6))],
+        )(*results)
     )
 
 

time: 106 us -> 105 us (level)
  no operation moved by 1% of the time
where the time goes in v5:
time: 105 us
  Pallas kernels  105 us (100%)
    pallas_call x1, Pallas kernels, shards(): pl.pallas_call(kernel, out_shape=outs, in_specs=[pl.BlockSpec(memory_spac...  102 us
    pallas_call x1, Pallas kernels, shards(): pl.pallas_call(hand_over, out_shape=outs, in_specs=[anywhere] * 4, out_sp...  2.59 us

profile of v5, /device:TPU:0, one launch (start us, length us, event | category | flops | bytes accessed | tf_op | source)
XLA Modules:
  0.0 105.2 jit_solution(5089891513242535816)
XLA Ops:
  0.6 102.0 %shard_map.111 = (bf16[32,6144]{1,0:T(8,128)(2,1)}, bf16[3,256,1024]{2,1,0:T(8,128)(2,1)}, f32[128,1024]{1,0:T(8,128)}, f32[3,3,1024]{2,1,0:T(4,128)}) custom-call(s32[32]{0:T(128)} %seg_ref.1, bf16[3,256,1024]{2,1,0:T(8,128)(2,1)} %proj_ref.1, f32[3,3,1024]{2,1,0:T(4,128)} %fw_ref.1, f32[128,1024]{1,0:T(8,128)} %lf_ref.1, bf16[1024,384]{1,0:T(8,128)(2,1)} %w_ref.1, ...), custom_call_target="tpu_custom_call" | custom-call | tf_op jit(solution)/shard_map/pallas_call | solution.py:835
  102.6 2.6 %shard_map.112 = (bf16[32,6144]{1,0:T(8,128)(2,1)}, bf16[3,256,1024]{2,1,0:T(8,128)(2,1)}, f32[128,1024]{1,0:T(8,128)}, f32[3,3,1024]{2,1,0:T(4,128)}) custom-call(bf16[32,6144]{1,0:T(8,128)(2,1)} %get-tuple-element.8.refs_0_, bf16[3,256,1024]{2,1,0:T(8,128)(2,1)} %get-tuple-element.9.refs_1_, f32[128,1024]{1,0:T(8,128)} %get-tuple-element.10.refs_2_, ...), custom_call_target="tpu_custom_call" | custom-call | tf_op jit(solution)/shard_map/pallas_call | solution.py:848
